TPU v7x, 512 devices: a whole 4x4x16 slice. The times are simulated.
512 devices in a mesh: wide: 32 (over x_lo, z), row: 4 (over y), col: 4 (over x_hi, core).
Axes of the slice: x: 4 (x_hi: 2, x_lo: 2; x = x_hi * 2 + x_lo), y: 4, z: 16, core: 2. Of those that a mesh axis runs over, the one named last changes fastest.
Arguments:
- tokens: bfloat16 [256, 12288], P('wide', ('row', 'col')), may hold values from -6 to 6
- in_weight: bfloat16 [12288, 24576], P(('row', 'col'), 'wide'), may hold values from -0.0546875 to 0.0546875
- out_weight: bfloat16 [24576, 12288], P('wide', ('row', 'col')), may hold values from -0.0390625 to 0.0390625
- out_grad: bfloat16 [256, 12288], P('wide', ('row', 'col')), may hold values from -1.5 to 1.5
Outputs:
- output: bfloat16 [256, 12288], P('wide', ('row', 'col'))
- tokens_grad: bfloat16 [256, 12288], P('wide', ('row', 'col'))
- in_weight_grad: bfloat16 [12288, 24576], P(('row', 'col'), 'wide')
- out_weight_grad: bfloat16 [24576, 12288], P('wide', ('row', 'col'))
All inputs are finite; a program needn't handle non-finite values.
Results may differ from a plain program's by a relative error of at most 0.005.
Values may be sent and summed in bfloat16 or wider, within the bound.
No kernel may reach another device: no remote copies, remote signals or barrier semaphores. Data moves between devices by JAX's collectives and lax.ppermute only.
A program may use at most 64 MiB of HBM per device.

v0:
```python
import jax
import jax.numpy as jnp
from jax import lax
from jax.sharding import PartitionSpec as P


def gelu_value(preact):
    inner_term = 0.7978845608028654 * (preact + 0.044715 * preact * preact * preact)
    return 0.5 * preact * (1.0 + jnp.tanh(inner_term))


def gelu_slope(preact):
    tangent = jnp.tanh(0.7978845608028654 * (preact + 0.044715 * preact * preact * preact))
    return 0.5 * (1.0 + tangent) + 0.5 * preact * (1.0 - tangent * tangent) * 0.7978845608028654 * (
        1.0 + 3.0 * 0.044715 * preact * preact
    )


def contract_first(left, right):
    return lax.dot_general(
        left, right, (((0,), (0,)), ((), ())), preferred_element_type=jnp.float32
    )


def contract_last(left, right):
    return lax.dot_general(
        left, right, (((1,), (1,)), ((), ())), preferred_element_type=jnp.float32
    )


def per_device(tokens, in_weight, out_weight, out_grad):
    gathered_inputs = lax.all_gather(tokens, "wide", axis=0, tiled=True)
    pre_part = jnp.dot(gathered_inputs, in_weight, preferred_element_type=jnp.float32)
    hidden_pre = lax.psum(pre_part, ("row", "col"))
    active = gelu_value(hidden_pre).astype(jnp.bfloat16)
    selected = active
    output = lax.psum_scatter(
        jnp.dot(selected, out_weight, preferred_element_type=jnp.float32),
        "wide",
        scatter_dimension=0,
        tiled=True,
    ).astype(jnp.bfloat16)
    gathered_grad = lax.all_gather(out_grad, "wide", axis=0, tiled=True)
    grad_part = contract_last(gathered_grad, out_weight)
    out_weight_grad = contract_first(active, gathered_grad).astype(jnp.bfloat16)
    grad_active = lax.psum(grad_part, ("row", "col"))
    grad_pre = (grad_active * gelu_slope(hidden_pre)).astype(jnp.bfloat16)
    in_weight_grad = contract_first(gathered_inputs, grad_pre)
    selected = grad_pre
    tokens_grad = lax.psum_scatter(
        contract_last(selected, in_weight), "wide", scatter_dimension=0, tiled=True
    ).astype(jnp.bfloat16)
    return (output, tokens_grad, in_weight_grad.astype(jnp.bfloat16), out_weight_grad)


def solution(mesh):
    in_specs = (
        P("wide", ("row", "col")),
        P(("row", "col"), "wide"),
        P("wide", ("row", "col")),
        P("wide", ("row", "col")),
    )
    out_specs = (
        P("wide", ("row", "col")),
        P("wide", ("row", "col")),
        P(("row", "col"), "wide"),
        P("wide", ("row", "col")),
    )
    return jax.shard_map(
        per_device, mesh=mesh, in_specs=in_specs, out_specs=out_specs, check_vma=False
    )
```

profile of v0, /device:TPU:24, one launch (start us, length us, event | category | flops | bytes accessed | tf_op | source)
XLA Modules:
  0.0 570.7 jit_solution(8403947291297761561)
XLA Ops:
  7.2 0.0 copy-start
  7.2 0.0 all-reduce.3.cloned.1.call-start
  7.2 71.2 %all_gather.6 = bf16[256,768]{1,0:T(8,128)(2,1)S(1)} all-gather(bf16[8,768]{1,0:T(8,128)(2,1)} %param.4), channel_id=1, replica_groups=mesh['wide'=32,'row'=4,'col'=4] {'wide'}, dimensions={0}, use_global_device_ids=true | all-gather | bytes 405504 | tf_op jit(solution)/shard_map/all_gather | solution.py:32
  78.5 60.9 %all_gather.7 = bf16[256,768]{1,0:T(8,128)(2,1)S(1)} all-gather(bf16[8,768]{1,0:T(8,128)(2,1)} %param.7), channel_id=1, replica_groups=mesh['wide'=32,'row'=4,'col'=4] {'wide'}, dimensions={0}, use_global_device_ids=true | all-gather | bytes 405504 | tf_op jit(solution)/shard_map/all_gather | solution.py:43
  139.3 2.6 fusion.9
  142.0 0.0 copy-done
  142.0 1.4 fusion.10
  143.4 0.0 all-reduce.3.cloned.1.call-update
  143.4 0.0 reduce-scatter.3.cloned.1.call-start
  143.4 143.9 %all-reduce.3.cloned.1.call-done = (f32[256,768]{1,0:T(8,128)}, f32[256,768]{1,0:T(8,128)}) async-done(((f32[256,768]{1,0:T(8,128)}, f32[256,768]{1,0:T(8,128)}), (f32[256,768]{1,0:T(8,128)}, f32[256,768]{1,0:T(8,128)})) %all-reduce.3.cloned.1.call-update) | async-done | bytes 1572880 | tf_op jit(solution)/shard_map/psum | solution.py:34
  287.4 2.6 fusion.8
  290.0 0.0 reduce-scatter.3.cloned.1.call-update
  290.0 0.0 copy-start.1
  290.0 0.0 reduce-scatter.5.cloned.1.call-start
  290.1 2.0 fusion.7
  292.1 0.0 copy-done.1
  292.1 1.4 fusion.11
  293.5 0.0 reduce-scatter.5.cloned.1.call-update
  293.5 0.5 fusion
  294.0 1.5 copy.8
  295.5 2.9 convolution_convert_fusion
  298.3 135.2 %reduce-scatter.3.cloned.1.call-done = f32[8,768]{1,0:T(8,128)} async-done(((f32[256,768]{1,0:T(8,128)}), f32[8,768]{1,0:T(8,128)}) %reduce-scatter.3.cloned.1.call-update) | async-done | bytes 24592 | tf_op jit(solution)/shard_map/reduce_scatter | solution.py:37
  433.5 1.3 convert_element_type.22
  434.8 128.0 %reduce-scatter.5.cloned.1.call-done = f32[8,768]{1,0:T(8,128)} async-done(((f32[256,768]{1,0:T(8,128)}), f32[8,768]{1,0:T(8,128)}) %reduce-scatter.5.cloned.1.call-update) | async-done | bytes 24592 | tf_op jit(solution)/shard_map/reduce_scatter | solution.py:50
  562.9 1.3 convert_element_type.24
Async XLA Ops:
  7.2 134.8 %copy-start = (bf16[768,768]{1,0:T(8,128)(2,1)S(1)}, bf16[768,768]{1,0:T(8,128)(2,1)}, u32[]{:S(2)}) copy-start(bf16[768,768]{1,0:T(8,128)(2,1)} %param.6) | copy-start | bytes 3538948
  7.2 280.2 %all-reduce.3.cloned.1.call-start = ((), (), s32[]{:S(2)}) async-start(), calls=%async_computation.4 | async-start | bytes 3145728 | tf_op jit(solution)/shard_map/psum | solution.py:34
  143.4 290.1 %reduce-scatter.3.cloned.1.call-start = ((), (), s32[]{:S(2)}) async-start(), calls=%async_computation.2 | async-start | bytes 811008 | tf_op jit(solution)/shard_map/reduce_scatter | solution.py:37
  290.0 2.0 copy-start.1
  290.0 272.8 %reduce-scatter.5.cloned.1.call-start = ((), (), s32[]{:S(2)}) async-start(), calls=%async_computation.3 | async-start | bytes 811008 | tf_op jit(solution)/shard_map/reduce_scatter | solution.py:50
Sparse Core Ops, SparseCore 0:
  143.5 143.8 all-reduce.2
  290.4 143.0 reduce-scatter.2
  436.3 126.5 reduce-scatter.4
where the time goes:
time: 571 us
  waiting for transfers between devices  407 us (71%)
  blocking collectives  132 us (23%)
  between operations  13.8 us (2%)
  matrix products  11.4 us (2%)
    psum x1, waiting for transfers between devices, per_device(): hidden_pre = lax.psum(pre_part, ('row', 'col'))  144 us
    reduce_scatter x1, waiting for transfers between devices, per_device(): lax.psum_scatter(jnp.dot(selected, out_weight, preferred_element_type=jnp...  135 us
    reduce_scatter x1, waiting for transfers between devices, per_device(): lax.psum_scatter(contract_last(selected, in_weight), 'wide', scatter_dime...  128 us
    all_gather x1, blocking collectives, per_device(): gathered_inputs = lax.all_gather(tokens, 'wide', axis=0, tiled=True)  71.2 us
    all_gather x1, blocking collectives, per_device(): gathered_grad = lax.all_gather(out_grad, 'wide', axis=0, tiled=True)  60.9 us
  transfers between devices with their start and end apart: 3, of which 3 were waited for; matrix products, arithmetic and copies ran while one was open for 2% of the time, Pallas kernels for 0%

commit v1 on v0

v1 whole, which is shorter than its diff:
```python
import jax
import jax.numpy as jnp
from jax import lax
from jax.sharding import Mesh
from jax.sharding import PartitionSpec as P

HIDDEN = ("y", "x_hi", "core")
C = 0.7978845608028654


def gelu_both(v):
    t = jnp.tanh(C * (v + 0.044715 * v * v * v))
    value = 0.5 * v * (1.0 + t)
    slope = 0.5 * (1.0 + t) + 0.5 * v * (1.0 - t * t) * C * (1.0 + 3.0 * 0.044715 * v * v)
    return value, slope


def dot(left, right, dims):
    return lax.dot_general(left, right, (dims, ((), ())), preferred_element_type=jnp.float32)


def per_device(tokens, in_weight, out_weight, out_grad):
    width = tokens.shape[1]
    parts = lax.axis_size(HIDDEN)
    both = jnp.concatenate([tokens, out_grad], axis=1)
    both = lax.all_gather(both, "x_lo", axis=0, tiled=True)
    both = lax.all_gather(both, "z", axis=0, tiled=True)
    all_tokens, all_grads = both[:, :width], both[:, width:]
    rows = both.shape[0]

    pre_part = dot(all_tokens, in_weight, ((1,), (0,))).astype(jnp.bfloat16)
    grad_part = dot(all_grads, out_weight, ((1,), (1,))).astype(jnp.bfloat16)
    sums = jnp.concatenate([pre_part, grad_part], axis=1).reshape(parts, rows // parts, -1)
    sums = lax.all_to_all(sums, HIDDEN, 0, 0, tiled=True)
    sums = jnp.sum(sums.astype(jnp.float32), axis=0)
    hidden = in_weight.shape[1]
    value, slope = gelu_both(sums[:, :hidden])
    share = jnp.concatenate([value, sums[:, hidden:] * slope], axis=1).astype(jnp.bfloat16)
    share = jnp.broadcast_to(share[None], (parts,) + share.shape)
    share = lax.all_to_all(share, HIDDEN, 0, 0, tiled=True).reshape(rows, -1)
    active, grad_pre = share[:, :hidden], share[:, hidden:]

    out_part = dot(active, out_weight, ((1,), (0,))).astype(jnp.bfloat16)
    back_part = dot(grad_pre, in_weight, ((1,), (1,))).astype(jnp.bfloat16)
    ends = jnp.concatenate([out_part, back_part], axis=1)
    group = lax.axis_size(("z", "x_lo"))
    ends = ends.reshape(group, rows // group, -1)
    ends = lax.all_to_all(ends, ("z", "x_lo"), 0, 0, tiled=True)
    out_weight_grad = dot(active, all_grads, ((0,), (0,))).astype(jnp.bfloat16)
    in_weight_grad = dot(all_tokens, grad_pre, ((0,), (0,))).astype(jnp.bfloat16)
    ends = jnp.sum(ends.astype(jnp.float32), axis=0).astype(jnp.bfloat16)
    return ends[:, :width], ends[:, width:], in_weight_grad, out_weight_grad


def solution(mesh):
    fine = Mesh(mesh.devices.reshape(2, -1, mesh.shape["row"], 2, 2), ("x_lo", "z", "y", "x_hi", "core"))
    wide = ("x_lo", "z")
    specs = (P(wide, HIDDEN), P(HIDDEN, wide), P(wide, HIDDEN), P(wide, HIDDEN))
    outs = (P(wide, HIDDEN), P(wide, HIDDEN), P(HIDDEN, wide), P(wide, HIDDEN))
    return jax.shard_map(per_device, mesh=fine, in_specs=specs, out_specs=outs, check_vma=False)
```

time: 571 us -> 143 us (0.25)
  waiting for transfers between devices: 407 us -> 40.7 us
  blocking collectives: 132 us -> 82.3 us
  between operations: 13.8 us -> 0.72 us
  starting transfers between devices: 0.12 us -> 6.83 us
    reduce_scatter x2 -> x0, waiting for transfers between devices: 263 us -> none  [the longest x1 135 us: per_device(): lax.psum_scatter(jnp.dot(selected, out_weight, preferred_element_type=jnp...]
    psum x1 -> x0, waiting for transfers between devices: 144 us -> none  [per_device(): hidden_pre = lax.psum(pre_part, ('row', 'col'))]
    all_gather x2, blocking collectives: 132 us -> 44.7 us  [the longest x1 40.3 us: per_device(): both = lax.all_gather(both, 'z', axis=0, tiled=True)]
    all_to_all x0 -> x1, waiting for transfers between devices: none -> 40.7 us  [per_device(): ends = lax.all_to_all(ends, ('z', 'x_lo'), 0, 0, tiled=True)]
    all_to_all x0 -> x2, blocking collectives: none -> 37.6 us  [the longest x1 19.9 us: per_device(): sums = lax.all_to_all(sums, HIDDEN, 0, 0, tiled=True)]
    all_to_all x0 -> x1, starting transfers between devices: none -> 6.83 us  [per_device(): ends = lax.all_to_all(ends, ('z', 'x_lo'), 0, 0, tiled=True)]
  transfers between devices with their start and end apart: 3 -> 1, of which waited for: 3 -> 1; matrix products, arithmetic and copies ran while one was open for 2% -> 2% of each run, Pallas kernels for 0% -> 0%
where the time goes in v1:
time: 143 us; the launch traced here: 140 us
  blocking collectives  82.3 us (58%)
  waiting for transfers between devices  40.7 us (28%)
  starting transfers between devices  6.83 us (5%)
  matrix products  6.28 us (4%)
  other arithmetic  2.1 us (1%)
  local copies, waits for them, and re-layouts  1.45 us (1%)
    all_to_all x1, waiting for transfers between devices, per_device(): ends = lax.all_to_all(ends, ('z', 'x_lo'), 0, 0, tiled=True)  40.7 us
    all_gather x1, blocking collectives, per_device(): both = lax.all_gather(both, 'z', axis=0, tiled=True)  40.3 us
    all_to_all x1, blocking collectives, per_device(): sums = lax.all_to_all(sums, HIDDEN, 0, 0, tiled=True)  19.9 us
    all_to_all x1, blocking collectives, per_device(): share = lax.all_to_all(share, HIDDEN, 0, 0, tiled=True).reshape(rows, -1)  17.7 us
    all_to_all x1, starting transfers between devices, per_device(): ends = lax.all_to_all(ends, ('z', 'x_lo'), 0, 0, tiled=True)  6.83 us
    dot_general x6, matrix products, dot(): lax.dot_general(left, right, (dims, ((), ())), preferred_element_type=jnp...  6.28 us
    all_gather x1, blocking collectives, per_device(): both = lax.all_gather(both, 'x_lo', axis=0, tiled=True)  4.49 us
  transfers between devices with their start and end apart: 1, of which 1 were waited for; matrix products, arithmetic and copies ran while one was open for 2% of the time, Pallas kernels for 0%

profile of v1, /device:TPU:24, one launch (start us, length us, event | category | flops | bytes accessed | tf_op | source)
XLA Modules:
  0.0 140.4 jit_solution(18327079976491467958)
XLA Ops:
  0.6 0.0 copy-start
  0.6 0.8 pad_maximum_fusion.2
  1.5 4.5 %all_gather.6 = bf16[16,1536]{1,0:T(8,128)(2,1)S(1)} all-gather(bf16[8,1536]{1,0:T(8,128)(2,1)S(1)} %pad_maximum_fusion.2), channel_id=1, replica_groups=mesh['x_lo'=2,'z'=16,'y'=4,'x_hi'=2,'core'=2] {'x_lo'}, dimensions={0}, use_global_device_ids=true | all-gather | bytes 73728 | tf_op jit(solution)/shard_map/all_gather | solution.py:26
  6.0 40.3 %all_gather.7 = bf16[256,1536]{1,0:T(8,128)(2,1)S(1)} all-gather(bf16[16,1536]{1,0:T(8,128)(2,1)S(1)} %all_gather.6), channel_id=1, replica_groups=mesh['x_lo'=2,'z'=16,'y'=4,'x_hi'=2,'core'=2] {'z'}, dimensions={0}, use_global_device_ids=true | all-gather | bytes 835584 | tf_op jit(solution)/shard_map/all_gather | solution.py:27
  46.2 1.8 %convolution_convert_fusion.4 = bf16[256,768]{1,0:T(8,128)(2,1)S(1)} fusion(bf16[768,768]{1,0:T(8,128)(2,1)} %param.6, bf16[256,1536]{1,0:T(8,128)(2,1)S(1)} %all_gather.7), kind=kOutput, calls=%fused_computation.5 | convolution fusion | flops 302186496 | bytes 1966080 | tf_op jit(solution)/shard_map/dot_general | solution.py:19
  48.0 0.0 copy-done
  48.0 0.5 convolution_convert_fusion.5
  48.5 0.1 pad_maximum_fusion
  48.5 19.9 %all_to_all.15 = bf16[16,16,1536]{2,1,0:T(8,128)(2,1)S(1)} all-to-all(bf16[16,16,1536]{2,1,0:T(8,128)(2,1)S(1)} %bitcast.8), channel_id=1, replica_groups=mesh['x_lo'=2,'z'=16,'y'=4,'x_hi'=2,'core'=2] {'y','x_hi','core'}, dimensions={0} | all-to-all | bytes 1572864 | tf_op jit(solution)/shard_map/all_to_all | solution.py:34
  68.4 0.1 convert_reduce_fusion
  68.6 0.1 broadcast_in_dim.2
  68.7 17.7 %all_to_all.16 = bf16[16,16,1536]{2,1,0:T(8,128)(2,1)S(1)} all-to-all(bf16[16,16,1536]{2,1,0:T(8,128)(2,1)S(1)} %broadcast_in_dim.2), channel_id=1, replica_groups=mesh['x_lo'=2,'z'=16,'y'=4,'x_hi'=2,'core'=2] {'y','x_hi','core'}, dimensions={0} | all-to-all | bytes 1572864 | tf_op jit(solution)/shard_map/all_to_all | solution.py:40
  86.4 0.0 copy-start.1
  86.4 0.5 convolution_convert_fusion.2
  86.9 0.8 copy-done.1
  87.7 0.5 convolution_convert_fusion.3
  88.2 0.9 maximum_bitcast_fusion
  89.1 6.8 %all-to-all-start.2 = ((bf16[32,8,1536]{2,1,0:T(8,128)(2,1)}), bf16[32,8,1536]{2,1,0:T(8,128)(2,1)S(1)}, u32[]{:S(2)}, u32[]{:S(2)}) async-start(bf16[32,8,1536]{2,1,0:T(8,128)(2,1)} %maximum_bitcast_fusion), calls=%async_computation.2 | async-start | bytes 1572864 | tf_op jit(solution)/shard_map/all_to_all | solution.py:48
  95.9 1.5 %convolution_convert_fusion = bf16[768,768]{1,0:T(8,128)(2,1)} fusion(bf16[256,1536]{1,0:T(8,128)(2,1)S(1)} %bitcast.11, bf16[256,1536]{1,0:T(8,128)(2,1)S(1)} %all_gather.7), kind=kOutput, calls=%fused_computation.1 | convolution fusion | flops 302579712 | bytes 1966080 | tf_op jit(solution)/shard_map/dot_general | solution.py:19
  97.5 1.5 %convolution_convert_fusion.1 = bf16[768,768]{1,0:T(8,128)(2,1)} fusion(bf16[256,1536]{1,0:T(8,128)(2,1)S(1)} %bitcast.12, bf16[256,1536]{1,0:T(8,128)(2,1)S(1)} %all_gather.7), kind=kOutput, calls=%fused_computation.2 | convolution fusion | flops 302579712 | bytes 1966080 | tf_op jit(solution)/shard_map/dot_general | solution.py:19
  99.0 40.7 %all-to-all-done.2 = bf16[32,8,1536]{2,1,0:T(8,128)(2,1)S(1)} async-done(((bf16[32,8,1536]{2,1,0:T(8,128)(2,1)}), bf16[32,8,1536]{2,1,0:T(8,128)(2,1)S(1)}, u32[]{:S(2)}, u32[]{:S(2)}) %all-to-all-start.2) | async-done | bytes 786464 | tf_op jit(solution)/shard_map/all_to_all | solution.py:48
  139.6 0.1 reduce_sum.22
  139.8 0.6 fusion.15
  (2 shorter events, 0.1 us)
Async XLA Ops:
  0.6 47.4 %copy-start = (bf16[768,768]{1,0:T(8,128)(2,1)S(1)}, bf16[768,768]{1,0:T(8,128)(2,1)}, u32[]{:S(2)}) copy-start(bf16[768,768]{1,0:T(8,128)(2,1)} %param.5) | copy-start | bytes 3538948
  86.4 1.3 copy-start.1
  89.1 50.5 %all-to-all-start.2 = ((bf16[32,8,1536]{2,1,0:T(8,128)(2,1)}), bf16[32,8,1536]{2,1,0:T(8,128)(2,1)S(1)}, u32[]{:S(2)}, u32[]{:S(2)}) async-start(bf16[32,8,1536]{2,1,0:T(8,128)(2,1)} %maximum_bitcast_fusion), calls=%async_computation.2 | async-start | bytes 1572864 | tf_op jit(solution)/shard_map/all_to_all | solution.py:48

commit v2 on v1

v2 whole, which is shorter than its diff:
```python
import jax
import jax.numpy as jnp
from jax import lax
from jax.sharding import Mesh
from jax.sharding import PartitionSpec as P

HIDDEN = ("y", "x_hi", "core")
NEAR = ("z_lo", "x_lo")
FAR = ("z_hi",)
C = 0.7978845608028654


def gelu_both(v):
    t = jnp.tanh(C * (v + 0.044715 * v * v * v))
    value = 0.5 * v * (1.0 + t)
    slope = 0.5 * (1.0 + t) + 0.5 * v * (1.0 - t * t) * C * (1.0 + 3.0 * 0.044715 * v * v)
    return value, slope


def dot(left, right, dims):
    return lax.dot_general(left, right, (dims, ((), ())), preferred_element_type=jnp.float32)


def gather(rows, axes):
    copies = jnp.broadcast_to(rows[None], (lax.axis_size(axes),) + rows.shape)
    return lax.all_to_all(copies, axes, 0, 0, tiled=True).reshape(-1, rows.shape[1])


def spread_sum(part, axes):
    blocks = part.reshape(lax.axis_size(axes), -1, part.shape[1])
    return jnp.sum(lax.all_to_all(blocks, axes, 0, 0, tiled=True).astype(jnp.float32), axis=0)


def per_device(tokens, in_weight, out_weight, out_grad):
    width = tokens.shape[1]
    both = jnp.concatenate([tokens, out_grad], axis=1)
    both = gather(gather(both, FAR), NEAR)
    all_tokens, all_grads = both[:, :width], both[:, width:]

    pre_part = dot(all_tokens, in_weight, ((1,), (0,))).astype(jnp.bfloat16)
    grad_part = dot(all_grads, out_weight, ((1,), (1,))).astype(jnp.bfloat16)
    sums = spread_sum(jnp.concatenate([pre_part, grad_part], axis=1), HIDDEN)
    hidden = in_weight.shape[1]
    value, slope = gelu_both(sums[:, :hidden])
    share = jnp.concatenate([value, sums[:, hidden:] * slope], axis=1).astype(jnp.bfloat16)
    share = gather(share, HIDDEN)
    active, grad_pre = share[:, :hidden], share[:, hidden:]

    out_part = dot(active, out_weight, ((1,), (0,))).astype(jnp.bfloat16)
    back_part = dot(grad_pre, in_weight, ((1,), (1,))).astype(jnp.bfloat16)
    ends = spread_sum(jnp.concatenate([out_part, back_part], axis=1), NEAR)
    out_weight_grad = dot(active, all_grads, ((0,), (0,))).astype(jnp.bfloat16)
    in_weight_grad = dot(all_tokens, grad_pre, ((0,), (0,))).astype(jnp.bfloat16)
    ends = spread_sum(ends, FAR).astype(jnp.bfloat16)
    return ends[:, :width], ends[:, width:], in_weight_grad, out_weight_grad


def solution(mesh):
    fine = Mesh(mesh.devices.reshape(2, -1, 4, mesh.shape["row"], 2, 2), ("x_lo", "z_hi", "z_lo", "y", "x_hi", "core"))
    wide = ("x_lo", "z_hi", "z_lo")
    specs = (P(wide, HIDDEN), P(HIDDEN, wide), P(wide, HIDDEN), P(wide, HIDDEN))
    outs = (P(wide, HIDDEN), P(wide, HIDDEN), P(HIDDEN, wide), P(wide, HIDDEN))
    return jax.shard_map(per_device, mesh=fine, in_specs=specs, out_specs=outs, check_vma=False)
```

time: 143 us -> 139 us (0.972)
  the two profiles are of different devices: /device:TPU:24 before, /device:TPU:32 now
where the time goes in v2:
time: 139 us
  blocking collectives  113 us (81%)
  waiting for transfers between devices  14.2 us (10%)
  matrix products  5.01 us (4%)
  starting transfers between devices  3.36 us (2%)
  other arithmetic  1.88 us (1%)
    all_to_all x3, blocking collectives, gather(): lax.all_to_all(copies, axes, 0, 0, tiled=True).reshape(-1, rows.shape[1])  68.4 us
    all_to_all x2, blocking collectives, spread_sum(): lax.all_to_all(blocks, axes, 0, 0, tiled=True).astype(jnp.float32)  44.3 us
    all_to_all x1, waiting for transfers between devices, spread_sum(): lax.all_to_all(blocks, axes, 0, 0, tiled=True).astype(jnp.float32)  14.2 us
    dot_general x6, matrix products, dot(): lax.dot_general(left, right, (dims, ((), ())), preferred_element_type=jnp...  5.01 us
    all_to_all x1, starting transfers between devices, spread_sum(): lax.all_to_all(blocks, axes, 0, 0, tiled=True).astype(jnp.float32)  3.36 us
  transfers between devices with their start and end apart: 1, of which 1 were waited for; matrix products, arithmetic and copies ran while one was open for 2% of the time, Pallas kernels for 0%

profile of v2, /device:TPU:32, one launch (start us, length us, event | category | flops | bytes accessed | tf_op | source)
XLA Modules:
  0.0 138.6 jit_solution(13153289121685536171)
XLA Ops:
  0.6 0.0 copy-start
  0.6 0.8 pad_maximum_fusion.3
  1.5 27.6 %all_to_all.30 = bf16[4,8,1536]{2,1,0:T(8,128)(2,1)S(1)} all-to-all(bf16[4,8,1536]{2,1,0:T(8,128)(2,1)S(1)} %broadcast_in_dim.8), channel_id=1, replica_groups=mesh['x_lo'=2,'z_hi'=4,'z_lo'=4,'y'=4,'x_hi'=2,'core'=2] {'z_hi'}, dimensions={0} | all-to-all | bytes 196608 | tf_op jit(solution)/shard_map/all_to_all | solution.py:26
  29.1 0.0 copy-start.1
  29.1 0.1 broadcast_in_dim.10
  29.2 23.0 %all_to_all.31 = bf16[8,32,1536]{2,1,0:T(8,128)(2,1)S(1)} all-to-all(bf16[8,32,1536]{2,1,0:T(8,128)(2,1)S(1)} %broadcast_in_dim.10), channel_id=1, replica_groups=mesh['x_lo'=2,'z_hi'=4,'z_lo'=4,'y'=4,'x_hi'=2,'core'=2] {'z_lo','x_lo'}, dimensions={0} | all-to-all | bytes 1572864 | tf_op jit(solution)/shard_map/all_to_all | solution.py:26
  52.1 0.0 copy-done.1
  52.1 0.5 convolution_convert_fusion.4
  52.7 0.0 copy-done
  52.7 0.5 convolution_convert_fusion.5
  53.2 0.1 pad_maximum_fusion
  53.2 21.7 %all_to_all.32 = bf16[16,16,1536]{2,1,0:T(8,128)(2,1)S(1)} all-to-all(bf16[16,16,1536]{2,1,0:T(8,128)(2,1)S(1)} %bitcast.10), channel_id=1, replica_groups=mesh['x_lo'=2,'z_hi'=4,'z_lo'=4,'y'=4,'x_hi'=2,'core'=2] {'y','x_hi','co..., dimensions={0} | all-to-all | bytes 1572864 | tf_op jit(solution)/shard_map/all_to_all | solution.py:31
  74.9 0.1 convert_reduce_fusion.1
  75.1 0.1 broadcast_in_dim.22
  75.2 17.8 %all_to_all.33 = bf16[16,16,1536]{2,1,0:T(8,128)(2,1)S(1)} all-to-all(bf16[16,16,1536]{2,1,0:T(8,128)(2,1)S(1)} %broadcast_in_dim.22), channel_id=1, replica_groups=mesh['x_lo'=2,'z_hi'=4,'z_lo'=4,'y'=4,'x_hi'=2,'core'=2] {'y','x_hi','co..., dimensions={0} | all-to-all | bytes 1572864 | tf_op jit(solution)/shard_map/all_to_all | solution.py:26
  93.0 0.5 convolution_convert_fusion.2
  93.5 0.5 convolution_convert_fusion.3
  94.0 0.1 pad_maximum_fusion.1
  94.0 22.6 %all_to_all.34 = bf16[8,32,1536]{2,1,0:T(8,128)(2,1)S(1)} all-to-all(bf16[8,32,1536]{2,1,0:T(8,128)(2,1)S(1)} %bitcast.11), channel_id=1, replica_groups=mesh['x_lo'=2,'z_hi'=4,'z_lo'=4,'y'=4,'x_hi'=2,'core'=2] {'z_lo','x_lo'}, dimensions={0} | all-to-all | bytes 1572864 | tf_op jit(solution)/shard_map/all_to_all | solution.py:31
  116.6 0.8 convert_reduce_fusion
  117.4 3.4 %all-to-all-start.5 = ((f32[4,8,1536]{2,1,0:T(8,128)}), f32[4,8,1536]{2,1,0:T(8,128)S(1)}, u32[]{:S(2)}, u32[]{:S(2)}) async-start(f32[4,8,1536]{2,1,0:T(8,128)} %bitcast.5), calls=%async_computation.5 | async-start | bytes 393216 | tf_op jit(solution)/shard_map/all_to_all | solution.py:31
  120.8 1.5 %convolution_convert_fusion = bf16[768,768]{1,0:T(8,128)(2,1)} fusion(bf16[256,1536]{1,0:T(8,128)(2,1)S(1)} %bitcast.18, bf16[256,1536]{1,0:T(8,128)(2,1)S(1)} %bitcast.14), kind=kOutput, calls=%fused_computation.2 | convolution fusion | flops 302579712 | bytes 1966080 | tf_op jit(solution)/shard_map/dot_general | solution.py:21
  122.3 1.5 %convolution_convert_fusion.1 = bf16[768,768]{1,0:T(8,128)(2,1)} fusion(bf16[256,1536]{1,0:T(8,128)(2,1)S(1)} %bitcast.19, bf16[256,1536]{1,0:T(8,128)(2,1)S(1)} %bitcast.15), kind=kOutput, calls=%fused_computation.3 | convolution fusion | flops 302579712 | bytes 1966080 | tf_op jit(solution)/shard_map/dot_general | solution.py:21
  123.8 14.2 %all-to-all-done.5 = f32[4,8,1536]{2,1,0:T(8,128)S(1)} async-done(((f32[4,8,1536]{2,1,0:T(8,128)}), f32[4,8,1536]{2,1,0:T(8,128)S(1)}, u32[]{:S(2)}, u32[]{:S(2)}) %all-to-all-start.5) | async-done | bytes 196640 | tf_op jit(solution)/shard_map/all_to_all | solution.py:31
  138.0 0.6 fusion.15
  (4 shorter events, 0.1 us)
Async XLA Ops:
  0.6 52.0 %copy-start = (bf16[768,768]{1,0:T(8,128)(2,1)S(1)}, bf16[768,768]{1,0:T(8,128)(2,1)}, u32[]{:S(2)}) copy-start(bf16[768,768]{1,0:T(8,128)(2,1)} %param.5) | copy-start | bytes 3538948
  29.1 23.0 %copy-start.1 = (bf16[768,768]{1,0:T(8,128)(2,1)S(1)}, bf16[768,768]{1,0:T(8,128)(2,1)}, u32[]{:S(2)}) copy-start(bf16[768,768]{1,0:T(8,128)(2,1)} %param.6) | copy-start | bytes 3538948
  117.4 20.6 %all-to-all-start.5 = ((f32[4,8,1536]{2,1,0:T(8,128)}), f32[4,8,1536]{2,1,0:T(8,128)S(1)}, u32[]{:S(2)}, u32[]{:S(2)}) async-start(f32[4,8,1536]{2,1,0:T(8,128)} %bitcast.5), calls=%async_computation.5 | async-start | bytes 393216 | tf_op jit(solution)/shard_map/all_to_all | solution.py:31

commit v3 on v2

--- a/solution.py
+++ b/solution.py
@@ -5,8 +5,9 @@
 from jax.sharding import PartitionSpec as P
 
 HIDDEN = ("y", "x_hi", "core")
-NEAR = ("z_lo", "x_lo")
-FAR = ("z_hi",)
+ORDER = ("core", "y", "x_hi")
+NEAR = ("x_lo", "z_near")
+FAR = ("z_far",)
 C = 0.7978845608028654
 
 
@@ -39,16 +40,16 @@
 
     pre_part = dot(all_tokens, in_weight, ((1,), (0,))).astype(jnp.bfloat16)
     grad_part = dot(all_grads, out_weight, ((1,), (1,))).astype(jnp.bfloat16)
-    sums = spread_sum(jnp.concatenate([pre_part, grad_part], axis=1), HIDDEN)
+    sums = spread_sum(jnp.concatenate([pre_part, grad_part], axis=1), ORDER)
     hidden = in_weight.shape[1]
     value, slope = gelu_both(sums[:, :hidden])
     share = jnp.concatenate([value, sums[:, hidden:] * slope], axis=1).astype(jnp.bfloat16)
-    share = gather(share, HIDDEN)
+    share = lax.all_gather(gather(share, ORDER[1:]), ORDER[0], axis=0, tiled=True)
     active, grad_pre = share[:, :hidden], share[:, hidden:]
 
     out_part = dot(active, out_weight, ((1,), (0,))).astype(jnp.bfloat16)
     back_part = dot(grad_pre, in_weight, ((1,), (1,))).astype(jnp.bfloat16)
-    ends = spread_sum(jnp.concatenate([out_part, back_part], axis=1), NEAR)
+    ends = spread_sum(jnp.concatenate([out_part, back_part], axis=1), NEAR).astype(jnp.bfloat16)
     out_weight_grad = dot(active, all_grads, ((0,), (0,))).astype(jnp.bfloat16)
     in_weight_grad = dot(all_tokens, grad_pre, ((0,), (0,))).astype(jnp.bfloat16)
     ends = spread_sum(ends, FAR).astype(jnp.bfloat16)
@@ -56,8 +57,8 @@
 
 
 def solution(mesh):
-    fine = Mesh(mesh.devices.reshape(2, -1, 4, mesh.shape["row"], 2, 2), ("x_lo", "z_hi", "z_lo", "y", "x_hi", "core"))
-    wide = ("x_lo", "z_hi", "z_lo")
+    fine = Mesh(mesh.devices.reshape(2, -1, 2, mesh.shape["row"], 2, 2), ("x_lo", "z_far", "z_near", "y", "x_hi", "core"))
+    wide = ("x_lo", "z_far", "z_near")
     specs = (P(wide, HIDDEN), P(HIDDEN, wide), P(wide, HIDDEN), P(wide, HIDDEN))
     outs = (P(wide, HIDDEN), P(wide, HIDDEN), P(HIDDEN, wide), P(wide, HIDDEN))
     return jax.shard_map(per_device, mesh=fine, in_specs=specs, out_specs=outs, check_vma=False)

time: 139 us -> 125 us (0.90)
  the two profiles are of different devices: /device:TPU:32 before, /device:TPU:24 now
where the time goes in v3:
time: 125 us; the launch traced here: 123 us
  blocking collectives  93.9 us (75%)
  waiting for transfers between devices  14.9 us (12%)
  starting transfers between devices  5.95 us (5%)
  matrix products  5.01 us (4%)
  other arithmetic  1.94 us (2%)
    all_to_all x3, blocking collectives, gather(): lax.all_to_all(copies, axes, 0, 0, tiled=True).reshape(-1, rows.shape[1])  57.8 us
    all_to_all x2, blocking collectives, spread_sum(): lax.all_to_all(blocks, axes, 0, 0, tiled=True).astype(jnp.float32)  33.7 us
    all_to_all x1, waiting for transfers between devices, spread_sum(): lax.all_to_all(blocks, axes, 0, 0, tiled=True).astype(jnp.float32)  14.9 us
    all_to_all x1, starting transfers between devices, spread_sum(): lax.all_to_all(blocks, axes, 0, 0, tiled=True).astype(jnp.float32)  5.95 us
    dot_general x6, matrix products, dot(): lax.dot_general(left, right, (dims, ((), ())), preferred_element_type=jnp...  5.01 us
  transfers between devices with their start and end apart: 1, of which 1 were waited for; matrix products, arithmetic and copies ran while one was open for 2% of the time, Pallas kernels for 0%

profile of v3, /device:TPU:24, one launch (start us, length us, event | category | flops | bytes accessed | tf_op | source)
XLA Modules:
  0.0 123.2 jit_solution(18398949938162683115)
XLA Ops:
  0.6 0.0 copy-start
  0.6 0.8 pad_maximum_fusion.3
  1.5 33.6 %all_to_all.30 = bf16[8,8,1536]{2,1,0:T(8,128)(2,1)S(1)} all-to-all(bf16[8,8,1536]{2,1,0:T(8,128)(2,1)S(1)} %broadcast_in_dim.8), channel_id=1, replica_groups=mesh['x_lo'=2,'z_far'=8,'z_near'=2,'y'=4,'x_hi'=2,'core'=2] {'z_far'}, dimensions={0} | all-to-all | bytes 393216 | tf_op jit(solution)/shard_map/all_to_all | solution.py:27
  35.0 0.0 copy-start.1
  35.0 0.1 broadcast_in_dim.10
  35.1 11.2 %all_to_all.31 = bf16[4,64,1536]{2,1,0:T(8,128)(2,1)S(1)} all-to-all(bf16[4,64,1536]{2,1,0:T(8,128)(2,1)S(1)} %broadcast_in_dim.10), channel_id=1, replica_groups=mesh['x_lo'=2,'z_far'=8,'z_near'=2,'y'=4,'x_hi'=2,'core'=2] {'x_lo','z_n..., dimensions={0} | all-to-all | bytes 1572864 | tf_op jit(solution)/shard_map/all_to_all | solution.py:27
  46.3 0.0 copy-done.1
  46.3 0.5 convolution_convert_fusion.4
  46.8 0.0 copy-done
  46.9 0.5 convolution_convert_fusion.5
  47.3 0.1 pad_maximum_fusion
  47.4 19.4 %all_to_all.32 = bf16[16,16,1536]{2,1,0:T(8,128)(2,1)S(1)} all-to-all(bf16[16,16,1536]{2,1,0:T(8,128)(2,1)S(1)} %bitcast.10), channel_id=1, replica_groups=mesh['x_lo'=2,'z_far'=8,'z_near'=2,'y'=4,'x_hi'=2,'core'=2] {'core','y',..., dimensions={0} | all-to-all | bytes 1572864 | tf_op jit(solution)/shard_map/all_to_all | solution.py:32
  66.8 0.1 convert_reduce_fusion
  67.0 13.1 %all_to_all.33 = bf16[8,16,1536]{2,1,0:T(8,128)(2,1)S(1)} all-to-all(bf16[8,16,1536]{2,1,0:T(8,128)(2,1)S(1)} %broadcast_in_dim.22), channel_id=1, replica_groups=mesh['x_lo'=2,'z_far'=8,'z_near'=2,'y'=4,'x_hi'=2,'core'=2] {'y','x_hi'}, dimensions={0} | all-to-all | bytes 786432 | tf_op jit(solution)/shard_map/all_to_all | solution.py:27
  80.1 2.4 %all_gather.3 = bf16[256,1536]{1,0:T(8,128)(2,1)S(1)} all-gather(bf16[128,1536]{1,0:T(8,128)(2,1)S(1)} %bitcast.16), channel_id=1, replica_groups=mesh['x_lo'=2,'z_far'=8,'z_near'=2,'y'=4,'x_hi'=2,'core'=2] {'core'}, dimensions={0}, use_global_device_ids=true | all-gather | bytes 1179648 | tf_op jit(solution)/shard_map/all_gather | solution.py:47
  82.4 0.5 convolution_convert_fusion.2
  83.0 0.5 convolution_convert_fusion.3
  83.4 0.1 pad_maximum_fusion.1
  83.5 14.3 %all_to_all.34 = bf16[4,64,1536]{2,1,0:T(8,128)(2,1)S(1)} all-to-all(bf16[4,64,1536]{2,1,0:T(8,128)(2,1)S(1)} %bitcast.11), channel_id=1, replica_groups=mesh['x_lo'=2,'z_far'=8,'z_near'=2,'y'=4,'x_hi'=2,'core'=2] {'x_lo','z_n..., dimensions={0} | all-to-all | bytes 1572864 | tf_op jit(solution)/shard_map/all_to_all | solution.py:32
  97.8 0.8 reduce_sum.34
  98.6 6.0 %all-to-all-start.5 = ((bf16[8,8,1536]{2,1,0:T(8,128)(2,1)}), bf16[8,8,1536]{2,1,0:T(8,128)(2,1)S(1)}, u32[]{:S(2)}, u32[]{:S(2)}) async-start(bf16[8,8,1536]{2,1,0:T(8,128)(2,1)} %bitcast.17), calls=%async_computation.5 | async-start | bytes 393216 | tf_op jit(solution)/shard_map/all_to_all | solution.py:32
  104.6 1.5 %convolution_convert_fusion = bf16[768,768]{1,0:T(8,128)(2,1)} fusion(bf16[256,1536]{1,0:T(8,128)(2,1)S(1)} %all_gather.3, bf16[256,1536]{1,0:T(8,128)(2,1)S(1)} %bitcast.14), kind=kOutput, calls=%fused_computation.1 | convolution fusion | flops 302579712 | bytes 1966080 | tf_op jit(solution)/shard_map/dot_general | solution.py:22
  106.1 1.5 %convolution_convert_fusion.1 = bf16[768,768]{1,0:T(8,128)(2,1)} fusion(bf16[256,1536]{1,0:T(8,128)(2,1)S(1)} %all_gather.3, bf16[256,1536]{1,0:T(8,128)(2,1)S(1)} %bitcast.15), kind=kOutput, calls=%fused_computation.2 | convolution fusion | flops 302579712 | bytes 1966080 | tf_op jit(solution)/shard_map/dot_general | solution.py:22
  107.6 14.9 %all-to-all-done.5 = bf16[8,8,1536]{2,1,0:T(8,128)(2,1)S(1)} async-done(((bf16[8,8,1536]{2,1,0:T(8,128)(2,1)}), bf16[8,8,1536]{2,1,0:T(8,128)(2,1)S(1)}, u32[]{:S(2)}, u32[]{:S(2)}) %all-to-all-start.5) | async-done | bytes 196640 | tf_op jit(solution)/shard_map/all_to_all | solution.py:32
  122.6 0.6 fusion.15
  (5 shorter events, 0.1 us)
Async XLA Ops:
  0.6 46.2 %copy-start = (bf16[768,768]{1,0:T(8,128)(2,1)S(1)}, bf16[768,768]{1,0:T(8,128)(2,1)}, u32[]{:S(2)}) copy-start(bf16[768,768]{1,0:T(8,128)(2,1)} %param.5) | copy-start | bytes 3538948
  35.0 11.3 %copy-start.1 = (bf16[768,768]{1,0:T(8,128)(2,1)S(1)}, bf16[768,768]{1,0:T(8,128)(2,1)}, u32[]{:S(2)}) copy-start(bf16[768,768]{1,0:T(8,128)(2,1)} %param.6) | copy-start | bytes 3538948
  98.6 23.9 %all-to-all-start.5 = ((bf16[8,8,1536]{2,1,0:T(8,128)(2,1)}), bf16[8,8,1536]{2,1,0:T(8,128)(2,1)S(1)}, u32[]{:S(2)}, u32[]{:S(2)}) async-start(bf16[8,8,1536]{2,1,0:T(8,128)(2,1)} %bitcast.17), calls=%async_computation.5 | async-start | bytes 393216 | tf_op jit(solution)/shard_map/all_to_all | solution.py:32

commit v4 on v3

--- a/solution.py
+++ b/solution.py
@@ -5,7 +5,7 @@
 from jax.sharding import PartitionSpec as P
 
 HIDDEN = ("y", "x_hi", "core")
-ORDER = ("core", "y", "x_hi")
+CHIPS = ("y", "x_hi")
 NEAR = ("x_lo", "z_near")
 FAR = ("z_far",)
 C = 0.7978845608028654
@@ -22,6 +22,10 @@
     return lax.dot_general(left, right, (dims, ((), ())), preferred_element_type=jnp.float32)
 
 
+def partner(rows, axes, k):
+    return lax.ppermute(rows, axes, [(i, i ^ k) for i in range(lax.axis_size(axes))])
+
+
 def gather(rows, axes):
     copies = jnp.broadcast_to(rows[None], (lax.axis_size(axes),) + rows.shape)
     return lax.all_to_all(copies, axes, 0, 0, tiled=True).reshape(-1, rows.shape[1])
@@ -32,24 +36,43 @@
     return jnp.sum(lax.all_to_all(blocks, axes, 0, 0, tiled=True).astype(jnp.float32), axis=0)
 
 
+def gather_near(rows):
+    others = [partner(rows, NEAR, k) for k in range(1, lax.axis_size(NEAR))]
+    return jnp.concatenate([rows] + others, axis=0)
+
+
+def sum_near(part):
+    blocks = jnp.split(part, lax.axis_size(NEAR), axis=0)
+    total = blocks[0].astype(jnp.float32)
+    for other in [partner(block, NEAR, k) for k, block in enumerate(blocks) if k]:
+        total = total + other.astype(jnp.float32)
+    return total
+
+
 def per_device(tokens, in_weight, out_weight, out_grad):
-    width = tokens.shape[1]
+    width, hidden = in_weight.shape
     both = jnp.concatenate([tokens, out_grad], axis=1)
-    both = gather(gather(both, FAR), NEAR)
+    both = gather_near(gather(both, FAR))
     all_tokens, all_grads = both[:, :width], both[:, width:]
 
-    pre_part = dot(all_tokens, in_weight, ((1,), (0,))).astype(jnp.bfloat16)
-    grad_part = dot(all_grads, out_weight, ((1,), (1,))).astype(jnp.bfloat16)
-    sums = spread_sum(jnp.concatenate([pre_part, grad_part], axis=1), ORDER)
-    hidden = in_weight.shape[1]
+    def hidden_part(half):
+        rows = both.shape[0] // 2
+        here = lax.dynamic_slice_in_dim(both, half * rows, rows, 0)
+        pre_part = dot(here[:, :width], in_weight, ((1,), (0,)))
+        grad_part = dot(here[:, width:], out_weight, ((1,), (1,)))
+        return jnp.concatenate([pre_part, grad_part], axis=1)
+
+    core = lax.axis_index("core")
+    other = partner(hidden_part(1 - core), "core", 1)
+    sums = spread_sum((hidden_part(core) + other).astype(jnp.bfloat16), CHIPS)
     value, slope = gelu_both(sums[:, :hidden])
     share = jnp.concatenate([value, sums[:, hidden:] * slope], axis=1).astype(jnp.bfloat16)
-    share = lax.all_gather(gather(share, ORDER[1:]), ORDER[0], axis=0, tiled=True)
+    share = lax.all_gather(gather(share, CHIPS), "core", axis=0, tiled=True)
     active, grad_pre = share[:, :hidden], share[:, hidden:]
 
     out_part = dot(active, out_weight, ((1,), (0,))).astype(jnp.bfloat16)
     back_part = dot(grad_pre, in_weight, ((1,), (1,))).astype(jnp.bfloat16)
-    ends = spread_sum(jnp.concatenate([out_part, back_part], axis=1), NEAR).astype(jnp.bfloat16)
+    ends = sum_near(jnp.concatenate([out_part, back_part], axis=1)).astype(jnp.bfloat16)
     out_weight_grad = dot(active, all_grads, ((0,), (0,))).astype(jnp.bfloat16)
     in_weight_grad = dot(all_tokens, grad_pre, ((0,), (0,))).astype(jnp.bfloat16)
     ends = spread_sum(ends, FAR).astype(jnp.bfloat16)

time: 125 us -> 129 us (1.032)
  blocking collectives: 93.9 us -> 63.1 us
  starting transfers between devices: 5.95 us -> 23.8 us
  waiting for transfers between devices: 14.9 us -> 27.9 us
  other arithmetic: 1.94 us -> 4.01 us
    ppermute x0 -> x7, starting transfers between devices: none -> 20.5 us  [partner(): lax.ppermute(rows, axes, [(i, i ^ k) for i in range(lax.axis_size(axes))])]
    all_to_all x2 -> x1, blocking collectives: 33.7 us -> 15 us  [spread_sum(): lax.all_to_all(blocks, axes, 0, 0, tiled=True).astype(jnp.float32)]
    ppermute x0 -> x7, waiting for transfers between devices: none -> 13.7 us  [partner(): lax.ppermute(rows, axes, [(i, i ^ k) for i in range(lax.axis_size(axes))])]
    all_to_all x3 -> x2, blocking collectives: 57.8 us -> 45.8 us  [gather(): lax.all_to_all(copies, axes, 0, 0, tiled=True).reshape(-1, rows.shape[1])]
    all_to_all x1, starting transfers between devices: 5.95 us -> 3.39 us  [spread_sum(): lax.all_to_all(blocks, axes, 0, 0, tiled=True).astype(jnp.float32)]
    dot_general x6 -> x8, matrix products: 5.01 us -> 5.76 us  [dot(): lax.dot_general(left, right, (dims, ((), ())), preferred_element_type=jnp...]
  transfers between devices with their start and end apart: 1 -> 8, of which waited for: 1 -> 5; matrix products, arithmetic and copies ran while one was open for 2% -> 3% of each run, Pallas kernels for 0% -> 0%
where the time goes in v4:
time: 129 us; the launch traced here: 127 us
  blocking collectives  63.1 us (49%)
  waiting for transfers between devices  27.9 us (22%)
  starting transfers between devices  23.8 us (18%)
  matrix products  5.76 us (4%)
  other arithmetic  4.01 us (3%)
  local copies, waits for them, and re-layouts  1.6 us (1%)
    all_to_all x2, blocking collectives, gather(): lax.all_to_all(copies, axes, 0, 0, tiled=True).reshape(-1, rows.shape[1])  45.8 us
    ppermute x7, starting transfers between devices, partner(): lax.ppermute(rows, axes, [(i, i ^ k) for i in range(lax.axis_size(axes))])  20.5 us
    all_to_all x1, blocking collectives, spread_sum(): lax.all_to_all(blocks, axes, 0, 0, tiled=True).astype(jnp.float32)  15 us
    all_to_all x1, waiting for transfers between devices, spread_sum(): lax.all_to_all(blocks, axes, 0, 0, tiled=True).astype(jnp.float32)  14.1 us
    ppermute x7, waiting for transfers between devices, partner(): lax.ppermute(rows, axes, [(i, i ^ k) for i in range(lax.axis_size(axes))])  13.7 us
    dot_general x8, matrix products, dot(): lax.dot_general(left, right, (dims, ((), ())), preferred_element_type=jnp...  5.76 us
    all_to_all x1, starting transfers between devices, spread_sum(): lax.all_to_all(blocks, axes, 0, 0, tiled=True).astype(jnp.float32)  3.39 us
  transfers between devices with their start and end apart: 8, of which 5 were waited for; matrix products, arithmetic and copies ran while one was open for 3% of the time, Pallas kernels for 0%

profile of v4, /device:TPU:24, one launch (start us, length us, event | category | flops | bytes accessed | tf_op | source)
XLA Modules:
  0.0 127.1 jit_solution(15952328212128928103)
XLA Ops:
  0.6 0.0 copy-start
  0.6 0.8 pad_maximum_fusion.4
  1.5 33.6 %all_to_all.20 = bf16[8,8,1536]{2,1,0:T(8,128)(2,1)S(1)} all-to-all(bf16[8,8,1536]{2,1,0:T(8,128)(2,1)S(1)} %broadcast_in_dim.4), channel_id=1, replica_groups=mesh['x_lo'=2,'z_far'=8,'z_near'=2,'y'=4,'x_hi'=2,'core'=2] {'z_far'}, dimensions={0} | all-to-all | bytes 393216 | tf_op jit(solution)/shard_map/all_to_all | solution.py:31
  35.0 2.4 %collective-permute-start = (bf16[64,1536]{1,0:T(8,128)(2,1)S(1)}, bf16[64,1536]{1,0:T(8,128)(2,1)S(1)}, u32[]{:S(2)}, u32[]{:S(2)}) collective-permute-start(bf16[64,1536]{1,0:T(8,128)(2,1)S(1)} %bitcast.13), channel_id=1, source_target_pairs={{0,16},{16,0},{256,272},{272,256},{1,17},{17,1},{257,273},{273,257... | collective-permute-start | bytes 589832 | tf_op jit(solution)/shard_map/ppermute | solution.py:26
  37.4 3.4 %collective-permute-start.1 = (bf16[64,1536]{1,0:T(8,128)(2,1)S(1)}, bf16[64,1536]{1,0:T(8,128)(2,1)S(1)}, u32[]{:S(2)}, u32[]{:S(2)}) collective-permute-start(bf16[64,1536]{1,0:T(8,128)(2,1)S(1)} %bitcast.14), channel_id=1, source_target_pairs={{0,256},{16,272},{256,0},{272,16},{1,257},{17,273},{257,1},{273,17... | collective-permute-start | bytes 589832 | tf_op jit(solution)/shard_map/ppermute | solution.py:26
  40.8 3.4 %collective-permute-start.2 = (bf16[64,1536]{1,0:T(8,128)(2,1)S(1)}, bf16[64,1536]{1,0:T(8,128)(2,1)S(1)}, u32[]{:S(2)}, u32[]{:S(2)}) collective-permute-start(bf16[64,1536]{1,0:T(8,128)(2,1)S(1)} %bitcast.15), channel_id=1, source_target_pairs={{0,272},{16,256},{256,16},{272,0},{1,273},{17,257},{257,17},{273,1... | collective-permute-start | bytes 589832 | tf_op jit(solution)/shard_map/ppermute | solution.py:26
  44.3 0.0 collective-permute-done
  44.3 2.3 %collective-permute-done.1 = bf16[64,1536]{1,0:T(8,128)(2,1)S(1)} collective-permute-done((bf16[64,1536]{1,0:T(8,128)(2,1)S(1)}, bf16[64,1536]{1,0:T(8,128)(2,1)S(1)}, u32[]{:S(2)}, u32[]{:S(2)}) %collective-permute-start.1) | collective-permute-done | bytes 196640 | tf_op jit(solution)/shard_map/ppermute | solution.py:26
  46.6 2.7 %collective-permute-done.2 = bf16[64,1536]{1,0:T(8,128)(2,1)S(1)} collective-permute-done((bf16[64,1536]{1,0:T(8,128)(2,1)S(1)}, bf16[64,1536]{1,0:T(8,128)(2,1)S(1)}, u32[]{:S(2)}, u32[]{:S(2)}) %collective-permute-start.2) | collective-permute-done | bytes 196640 | tf_op jit(solution)/shard_map/ppermute | solution.py:26
  49.3 0.1 pad_maximum_fusion
  49.4 0.0 copy-done
  49.4 0.0 copy-start.1
  49.4 0.3 fusion.13
  49.7 0.9 copy-done.1
  50.6 0.5 fusion.11
  51.2 1.0 pad_maximum_fusion.1
  52.1 1.9 %collective-permute-start.3 = (f32[128,1536]{1,0:T(8,128)}, f32[128,1536]{1,0:T(8,128)}, u32[]{:S(2)}, u32[]{:S(2)}) collective-permute-start(f32[128,1536]{1,0:T(8,128)} %pad_maximum_fusion.1), channel_id=1, source_target_pairs={{0,1},{1,0},{2,3},{3,2},{4,5},{5,4},{6,7},{7,6},{8,9},{9,8},{10,11... | collective-permute-start | bytes 2359304 | tf_op jit(solution)/shard_map/ppermute | solution.py:26
  54.1 0.5 fusion.15
  54.6 0.3 fusion.17
  54.9 1.7 %collective-permute-done.3 = f32[128,1536]{1,0:T(8,128)} collective-permute-done((f32[128,1536]{1,0:T(8,128)}, f32[128,1536]{1,0:T(8,128)}, u32[]{:S(2)}, u32[]{:S(2)}) %collective-permute-start.3) | collective-permute-done | bytes 786464 | tf_op jit(solution)/shard_map/ppermute | solution.py:26
  56.7 1.2 fusion
  57.9 15.0 %all_to_all.21 = bf16[8,16,1536]{2,1,0:T(8,128)(2,1)S(1)} all-to-all(bf16[8,16,1536]{2,1,0:T(8,128)(2,1)S(1)} %bitcast.12), channel_id=1, replica_groups=mesh['x_lo'=2,'z_far'=8,'z_near'=2,'y'=4,'x_hi'=2,'core'=2] {'y','x_hi'}, dimensions={0} | all-to-all | bytes 786432 | tf_op jit(solution)/shard_map/all_to_all | solution.py:36
  72.9 0.1 convert_reduce_fusion
  73.0 12.2 %all_to_all.22 = bf16[8,16,1536]{2,1,0:T(8,128)(2,1)S(1)} all-to-all(bf16[8,16,1536]{2,1,0:T(8,128)(2,1)S(1)} %broadcast_in_dim.5), channel_id=1, replica_groups=mesh['x_lo'=2,'z_far'=8,'z_near'=2,'y'=4,'x_hi'=2,'core'=2] {'y','x_hi'}, dimensions={0} | all-to-all | bytes 786432 | tf_op jit(solution)/shard_map/all_to_all | solution.py:31
  85.3 2.4 %all_gather.3 = bf16[256,1536]{1,0:T(8,128)(2,1)S(1)} all-gather(bf16[128,1536]{1,0:T(8,128)(2,1)S(1)} %bitcast.11), channel_id=1, replica_groups=mesh['x_lo'=2,'z_far'=8,'z_near'=2,'y'=4,'x_hi'=2,'core'=2] {'core'}, dimensions={0}, use_global_device_ids=true | all-gather | bytes 1179648 | tf_op jit(solution)/shard_map/all_gather | solution.py:70
  87.6 0.0 copy-start.2
  87.6 0.5 convolution_convert_fusion.2
  88.1 0.5 convolution_convert_fusion.3
  88.6 0.0 copy-done.2
  88.7 0.0 copy-start.3
  88.7 3.6 %collective-permute-start.4 = (bf16[64,1536]{1,0:T(8,128)(2,1)S(1)}, bf16[64,1536]{1,0:T(8,128)(2,1)S(1)}, u32[]{:S(2)}, u32[]{:S(2)}) collective-permute-start(bf16[64,1536]{1,0:T(8,128)(2,1)S(1)} %get-tuple-element.4), channel_id=1, source_target_pairs={{0,16},{16,0},{256,272},{272,256},{1,17},{17,1},{257,273},{273,257... | collective-permute-start | bytes 589832 | tf_op jit(solution)/shard_map/ppermute | solution.py:26
  92.3 2.1 %collective-permute-start.5 = (bf16[64,1536]{1,0:T(8,128)(2,1)S(1)}, bf16[64,1536]{1,0:T(8,128)(2,1)S(1)}, u32[]{:S(2)}, u32[]{:S(2)}) collective-permute-start(bf16[64,1536]{1,0:T(8,128)(2,1)S(1)} %get-tuple-element.6), channel_id=1, source_target_pairs={{0,256},{16,272},{256,0},{272,16},{1,257},{17,273},{257,1},{273,17... | collective-permute-start | bytes 589832 | tf_op jit(solution)/shard_map/ppermute | solution.py:26
  94.4 3.6 %collective-permute-start.6 = (bf16[64,1536]{1,0:T(8,128)(2,1)S(1)}, bf16[64,1536]{1,0:T(8,128)(2,1)S(1)}, u32[]{:S(2)}, u32[]{:S(2)}) collective-permute-start(bf16[64,1536]{1,0:T(8,128)(2,1)S(1)} %get-tuple-element.5), channel_id=1, source_target_pairs={{0,272},{16,256},{256,16},{272,0},{1,273},{17,257},{257,17},{273,1... | collective-permute-start | bytes 589832 | tf_op jit(solution)/shard_map/ppermute | solution.py:26
  98.0 0.0 collective-permute-done.4
  98.1 7.0 %collective-permute-done.5 = bf16[64,1536]{1,0:T(8,128)(2,1)S(1)} collective-permute-done((bf16[64,1536]{1,0:T(8,128)(2,1)S(1)}, bf16[64,1536]{1,0:T(8,128)(2,1)S(1)}, u32[]{:S(2)}, u32[]{:S(2)}) %collective-permute-start.5) | collective-permute-done | bytes 196640 | tf_op jit(solution)/shard_map/ppermute | solution.py:26
  105.0 0.0 collective-permute-done.6
  105.0 0.8 fusion.7
  105.8 3.4 %all-to-all-start.3 = ((bf16[8,8,1536]{2,1,0:T(8,128)(2,1)}), bf16[8,8,1536]{2,1,0:T(8,128)(2,1)S(1)}, u32[]{:S(2)}, u32[]{:S(2)}) async-start(bf16[8,8,1536]{2,1,0:T(8,128)(2,1)} %fusion.7), calls=%async_computation.3 | async-start | bytes 393216 | tf_op jit(solution)/shard_map/all_to_all | solution.py:36
  109.2 0.0 copy-done.3
  109.2 1.5 %convolution_convert_fusion = bf16[768,768]{1,0:T(8,128)(2,1)} fusion(bf16[256,1536]{1,0:T(8,128)(2,1)S(1)} %pad_maximum_fusion, bf16[256,1536]{1,0:T(8,128)(2,1)S(1)} %copy-done.3), kind=kOutput, calls=%fused_computation | convolution fusion | flops 302579712 | bytes 1966080 | tf_op jit(solution)/shard_map/dot_general | solution.py:22
  110.8 1.5 %convolution_convert_fusion.1 = bf16[768,768]{1,0:T(8,128)(2,1)} fusion(bf16[256,1536]{1,0:T(8,128)(2,1)S(1)} %pad_maximum_fusion, bf16[256,1536]{1,0:T(8,128)(2,1)S(1)} %copy-done.3), kind=kOutput, calls=%fused_computation.1 | convolution fusion | flops 302579712 | bytes 1966080 | tf_op jit(solution)/shard_map/dot_general | solution.py:22
  112.3 14.1 %all-to-all-done.3 = bf16[8,8,1536]{2,1,0:T(8,128)(2,1)S(1)} async-done(((bf16[8,8,1536]{2,1,0:T(8,128)(2,1)}), bf16[8,8,1536]{2,1,0:T(8,128)(2,1)S(1)}, u32[]{:S(2)}, u32[]{:S(2)}) %all-to-all-start.3) | async-done | bytes 196640 | tf_op jit(solution)/shard_map/all_to_all | solution.py:36
  126.5 0.6 fusion.28
  (6 shorter events, 0.2 us)
Async XLA Ops:
  0.6 48.7 %copy-start = (bf16[768,768]{1,0:T(8,128)(2,1)S(1)}, bf16[768,768]{1,0:T(8,128)(2,1)}, u32[]{:S(2)}) copy-start(bf16[768,768]{1,0:T(8,128)(2,1)} %param.5) | copy-start | bytes 3538948
  35.0 9.2 %collective-permute-start = (bf16[64,1536]{1,0:T(8,128)(2,1)S(1)}, bf16[64,1536]{1,0:T(8,128)(2,1)S(1)}, u32[]{:S(2)}, u32[]{:S(2)}) collective-permute-start(bf16[64,1536]{1,0:T(8,128)(2,1)S(1)} %bitcast.13), channel_id=1, source_target_pairs={{0,16},{16,0},{256,272},{272,256},{1,17},{17,1},{257,273},{273,257... | collective-permute-start | bytes 589832 | tf_op jit(solution)/shard_map/ppermute | solution.py:26
  37.4 9.1 %collective-permute-start.1 = (bf16[64,1536]{1,0:T(8,128)(2,1)S(1)}, bf16[64,1536]{1,0:T(8,128)(2,1)S(1)}, u32[]{:S(2)}, u32[]{:S(2)}) collective-permute-start(bf16[64,1536]{1,0:T(8,128)(2,1)S(1)} %bitcast.14), channel_id=1, source_target_pairs={{0,256},{16,272},{256,0},{272,16},{1,257},{17,273},{257,1},{273,17... | collective-permute-start | bytes 589832 | tf_op jit(solution)/shard_map/ppermute | solution.py:26
  40.8 8.5 %collective-permute-start.2 = (bf16[64,1536]{1,0:T(8,128)(2,1)S(1)}, bf16[64,1536]{1,0:T(8,128)(2,1)S(1)}, u32[]{:S(2)}, u32[]{:S(2)}) collective-permute-start(bf16[64,1536]{1,0:T(8,128)(2,1)S(1)} %bitcast.15), channel_id=1, source_target_pairs={{0,272},{16,256},{256,16},{272,0},{1,273},{17,257},{257,17},{273,1... | collective-permute-start | bytes 589832 | tf_op jit(solution)/shard_map/ppermute | solution.py:26
  49.4 1.3 %copy-start.1 = (bf16[768,768]{1,0:T(8,128)(2,1)S(1)}, bf16[768,768]{1,0:T(8,128)(2,1)}, u32[]{:S(2)}) copy-start(bf16[768,768]{1,0:T(8,128)(2,1)} %param.6) | copy-start | bytes 3538948
  52.1 4.5 %collective-permute-start.3 = (f32[128,1536]{1,0:T(8,128)}, f32[128,1536]{1,0:T(8,128)}, u32[]{:S(2)}, u32[]{:S(2)}) collective-permute-start(f32[128,1536]{1,0:T(8,128)} %pad_maximum_fusion.1), channel_id=1, source_target_pairs={{0,1},{1,0},{2,3},{3,2},{4,5},{5,4},{6,7},{7,6},{8,9},{9,8},{10,11... | collective-permute-start | bytes 2359304 | tf_op jit(solution)/shard_map/ppermute | solution.py:26
  87.6 1.0 copy-start.2
  88.7 20.6 %copy-start.3 = (bf16[256,1536]{1,0:T(8,128)(2,1)S(1)}, bf16[256,1536]{1,0:T(8,128)(2,1)}, u32[]{:S(2)}) copy-start(bf16[256,1536]{1,0:T(8,128)(2,1)} %copy-done.2) | copy-start | bytes 2359300
  88.7 9.4 %collective-permute-start.4 = (bf16[64,1536]{1,0:T(8,128)(2,1)S(1)}, bf16[64,1536]{1,0:T(8,128)(2,1)S(1)}, u32[]{:S(2)}, u32[]{:S(2)}) collective-permute-start(bf16[64,1536]{1,0:T(8,128)(2,1)S(1)} %get-tuple-element.4), channel_id=1, source_target_pairs={{0,16},{16,0},{256,272},{272,256},{1,17},{17,1},{257,273},{273,257... | collective-permute-start | bytes 589832 | tf_op jit(solution)/shard_map/ppermute | solution.py:26
  92.3 12.8 %collective-permute-start.5 = (bf16[64,1536]{1,0:T(8,128)(2,1)S(1)}, bf16[64,1536]{1,0:T(8,128)(2,1)S(1)}, u32[]{:S(2)}, u32[]{:S(2)}) collective-permute-start(bf16[64,1536]{1,0:T(8,128)(2,1)S(1)} %get-tuple-element.6), channel_id=1, source_target_pairs={{0,256},{16,272},{256,0},{272,16},{1,257},{17,273},{257,1},{273,17... | collective-permute-start | bytes 589832 | tf_op jit(solution)/shard_map/ppermute | solution.py:26
  94.4 10.6 %collective-permute-start.6 = (bf16[64,1536]{1,0:T(8,128)(2,1)S(1)}, bf16[64,1536]{1,0:T(8,128)(2,1)S(1)}, u32[]{:S(2)}, u32[]{:S(2)}) collective-permute-start(bf16[64,1536]{1,0:T(8,128)(2,1)S(1)} %get-tuple-element.5), channel_id=1, source_target_pairs={{0,272},{16,256},{256,16},{272,0},{1,273},{17,257},{257,17},{273,1... | collective-permute-start | bytes 589832 | tf_op jit(solution)/shard_map/ppermute | solution.py:26
  105.8 20.6 %all-to-all-start.3 = ((bf16[8,8,1536]{2,1,0:T(8,128)(2,1)}), bf16[8,8,1536]{2,1,0:T(8,128)(2,1)S(1)}, u32[]{:S(2)}, u32[]{:S(2)}) async-start(bf16[8,8,1536]{2,1,0:T(8,128)(2,1)} %fusion.7), calls=%async_computation.3 | async-start | bytes 393216 | tf_op jit(solution)/shard_map/all_to_all | solution.py:36

commit v5 on v3

--- a/solution.py
+++ b/solution.py
@@ -34,13 +34,19 @@
 
 def per_device(tokens, in_weight, out_weight, out_grad):
     width = tokens.shape[1]
+    first, tokens = lax.optimization_barrier((lax.axis_index("core") == 0, tokens))
     both = jnp.concatenate([tokens, out_grad], axis=1)
     both = gather(gather(both, FAR), NEAR)
     all_tokens, all_grads = both[:, :width], both[:, width:]
 
-    pre_part = dot(all_tokens, in_weight, ((1,), (0,))).astype(jnp.bfloat16)
-    grad_part = dot(all_grads, out_weight, ((1,), (1,))).astype(jnp.bfloat16)
-    sums = spread_sum(jnp.concatenate([pre_part, grad_part], axis=1), ORDER)
+    half = all_tokens.shape[0] // 2
+    pre_part = dot(all_tokens, in_weight, ((1,), (0,)))
+    grad_part = dot(all_grads, out_weight, ((1,), (1,)))
+    low = jnp.concatenate([pre_part[:half], grad_part[:half]], axis=1)
+    high = jnp.concatenate([pre_part[half:], grad_part[half:]], axis=1)
+    other = lax.all_gather(jnp.where(first, high, low).astype(jnp.bfloat16), "core", axis=0, tiled=True)
+    other = jnp.where(first, other[half:], other[:half]).astype(jnp.float32)
+    sums = spread_sum((jnp.where(first, low, high) + other).astype(jnp.bfloat16), ORDER[1:])
     hidden = in_weight.shape[1]
     value, slope = gelu_both(sums[:, :hidden])
     share = jnp.concatenate([value, sums[:, hidden:] * slope], axis=1).astype(jnp.bfloat16)

time: 125 us -> 122 us (0.976)
  blocking collectives: 93.9 us -> 91.2 us
    all_to_all x2, blocking collectives: 33.7 us -> 29.5 us  [spread_sum(): lax.all_to_all(blocks, axes, 0, 0, tiled=True).astype(jnp.float32)]
    all_gather x0 -> x1, blocking collectives: none -> 2.37 us  [per_device(): lax.all_gather(jnp.where(first, high, low).astype(jnp.bfloat16), 'core',...]
  transfers between devices with their start and end apart: 1 -> 1, of which waited for: 1 -> 1; matrix products, arithmetic and copies ran while one was open for 2% -> 3% of each run, Pallas kernels for 0% -> 0%
where the time goes in v5:
time: 122 us; the launch traced here: 121 us
  blocking collectives  91.2 us (75%)
  waiting for transfers between devices  14.9 us (12%)
  starting transfers between devices  5.95 us (5%)
  matrix products  5.01 us (4%)
  other arithmetic  2.05 us (2%)
    all_to_all x3, blocking collectives, gather(): lax.all_to_all(copies, axes, 0, 0, tiled=True).reshape(-1, rows.shape[1])  57 us
    all_to_all x2, blocking collectives, spread_sum(): lax.all_to_all(blocks, axes, 0, 0, tiled=True).astype(jnp.float32)  29.5 us
    all_to_all x1, waiting for transfers between devices, spread_sum(): lax.all_to_all(blocks, axes, 0, 0, tiled=True).astype(jnp.float32)  14.9 us
    all_to_all x1, starting transfers between devices, spread_sum(): lax.all_to_all(blocks, axes, 0, 0, tiled=True).astype(jnp.float32)  5.95 us
    dot_general x6, matrix products, dot(): lax.dot_general(left, right, (dims, ((), ())), preferred_element_type=jnp...  5.01 us
  transfers between devices with their start and end apart: 1, of which 1 were waited for; matrix products, arithmetic and copies ran while one was open for 3% of the time, Pallas kernels for 0%

profile of v5, /device:TPU:24, one launch (start us, length us, event | category | flops | bytes accessed | tf_op | source)
XLA Modules:
  0.0 120.7 jit_solution(9159122213395174620)
XLA Ops:
  0.6 0.0 copy-start
  0.7 0.8 pad_maximum_fusion.4
  1.5 33.6 %all_to_all.30 = bf16[8,8,1536]{2,1,0:T(8,128)(2,1)S(1)} all-to-all(bf16[8,8,1536]{2,1,0:T(8,128)(2,1)S(1)} %broadcast_in_dim.8), channel_id=1, replica_groups=mesh['x_lo'=2,'z_far'=8,'z_near'=2,'y'=4,'x_hi'=2,'core'=2] {'z_far'}, dimensions={0} | all-to-all | bytes 393216 | tf_op jit(solution)/shard_map/all_to_all | solution.py:27
  35.0 0.0 copy-start.1
  35.0 0.1 broadcast_in_dim.10
  35.1 11.2 %all_to_all.31 = bf16[4,64,1536]{2,1,0:T(8,128)(2,1)S(1)} all-to-all(bf16[4,64,1536]{2,1,0:T(8,128)(2,1)S(1)} %broadcast_in_dim.10), channel_id=1, replica_groups=mesh['x_lo'=2,'z_far'=8,'z_near'=2,'y'=4,'x_hi'=2,'core'=2] {'x_lo','z_n..., dimensions={0} | all-to-all | bytes 1572864 | tf_op jit(solution)/shard_map/all_to_all | solution.py:27
  46.3 0.0 copy-done.1
  46.3 0.5 fusion.5
  46.8 0.0 copy-done
  46.9 0.5 fusion.8
  47.3 0.1 fusion.17
  47.5 0.1 select_convert_fusion
  47.5 2.4 %all_gather.6 = bf16[256,1536]{1,0:T(8,128)(2,1)S(1)} all-gather(bf16[128,1536]{1,0:T(8,128)(2,1)S(1)} %select_convert_fusion), channel_id=1, replica_groups=mesh['x_lo'=2,'z_far'=8,'z_near'=2,'y'=4,'x_hi'=2,'core'=2] {'core'}, dimensions={0}, use_global_device_ids=true | all-gather | bytes 1179648 | tf_op jit(solution)/shard_map/all_gather | solution.py:47
  49.9 0.1 add_convert_fusion
  50.1 15.2 %all_to_all.32 = bf16[8,16,1536]{2,1,0:T(8,128)(2,1)S(1)} all-to-all(bf16[8,16,1536]{2,1,0:T(8,128)(2,1)S(1)} %bitcast.16), channel_id=1, replica_groups=mesh['x_lo'=2,'z_far'=8,'z_near'=2,'y'=4,'x_hi'=2,'core'=2] {'y','x_hi'}, dimensions={0} | all-to-all | bytes 786432 | tf_op jit(solution)/shard_map/all_to_all | solution.py:32
  65.2 0.1 convert_reduce_fusion
  65.4 12.2 %all_to_all.33 = bf16[8,16,1536]{2,1,0:T(8,128)(2,1)S(1)} all-to-all(bf16[8,16,1536]{2,1,0:T(8,128)(2,1)S(1)} %broadcast_in_dim.22), channel_id=1, replica_groups=mesh['x_lo'=2,'z_far'=8,'z_near'=2,'y'=4,'x_hi'=2,'core'=2] {'y','x_hi'}, dimensions={0} | all-to-all | bytes 786432 | tf_op jit(solution)/shard_map/all_to_all | solution.py:27
  77.6 2.4 %all_gather.7 = bf16[256,1536]{1,0:T(8,128)(2,1)S(1)} all-gather(bf16[128,1536]{1,0:T(8,128)(2,1)S(1)} %bitcast.15), channel_id=1, replica_groups=mesh['x_lo'=2,'z_far'=8,'z_near'=2,'y'=4,'x_hi'=2,'core'=2] {'core'}, dimensions={0}, use_global_device_ids=true | all-gather | bytes 1179648 | tf_op jit(solution)/shard_map/all_gather | solution.py:53
  80.0 0.5 convolution_convert_fusion.2
  80.5 0.5 convolution_convert_fusion.3
  80.9 0.1 pad_maximum_fusion.2
  81.0 14.3 %all_to_all.34 = bf16[4,64,1536]{2,1,0:T(8,128)(2,1)S(1)} all-to-all(bf16[4,64,1536]{2,1,0:T(8,128)(2,1)S(1)} %bitcast.14), channel_id=1, replica_groups=mesh['x_lo'=2,'z_far'=8,'z_near'=2,'y'=4,'x_hi'=2,'core'=2] {'x_lo','z_n..., dimensions={0} | all-to-all | bytes 1572864 | tf_op jit(solution)/shard_map/all_to_all | solution.py:32
  95.3 0.8 reduce_sum.34
  96.1 5.9 %all-to-all-start.5 = ((bf16[8,8,1536]{2,1,0:T(8,128)(2,1)}), bf16[8,8,1536]{2,1,0:T(8,128)(2,1)S(1)}, u32[]{:S(2)}, u32[]{:S(2)}) async-start(bf16[8,8,1536]{2,1,0:T(8,128)(2,1)} %bitcast.17), calls=%async_computation.5 | async-start | bytes 393216 | tf_op jit(solution)/shard_map/all_to_all | solution.py:32
  102.1 1.5 %convolution_convert_fusion = bf16[768,768]{1,0:T(8,128)(2,1)} fusion(bf16[256,1536]{1,0:T(8,128)(2,1)S(1)} %all_gather.7, bf16[256,1536]{1,0:T(8,128)(2,1)S(1)} %bitcast.12), kind=kOutput, calls=%fused_computation | convolution fusion | flops 302579712 | bytes 1966080 | tf_op jit(solution)/shard_map/dot_general | solution.py:22
  103.6 1.5 %convolution_convert_fusion.1 = bf16[768,768]{1,0:T(8,128)(2,1)} fusion(bf16[256,1536]{1,0:T(8,128)(2,1)S(1)} %all_gather.7, bf16[256,1536]{1,0:T(8,128)(2,1)S(1)} %bitcast.13), kind=kOutput, calls=%fused_computation.1 | convolution fusion | flops 302579712 | bytes 1966080 | tf_op jit(solution)/shard_map/dot_general | solution.py:22
  105.2 14.9 %all-to-all-done.5 = bf16[8,8,1536]{2,1,0:T(8,128)(2,1)S(1)} async-done(((bf16[8,8,1536]{2,1,0:T(8,128)(2,1)}), bf16[8,8,1536]{2,1,0:T(8,128)(2,1)S(1)}, u32[]{:S(2)}, u32[]{:S(2)}) %all-to-all-start.5) | async-done | bytes 196640 | tf_op jit(solution)/shard_map/all_to_all | solution.py:32
  120.1 0.6 fusion.19
  (5 shorter events, 0.1 us)
Async XLA Ops:
  0.6 46.2 %copy-start = (bf16[768,768]{1,0:T(8,128)(2,1)S(1)}, bf16[768,768]{1,0:T(8,128)(2,1)}, u32[]{:S(2)}) copy-start(bf16[768,768]{1,0:T(8,128)(2,1)} %param.5) | copy-start | bytes 3538948
  35.0 11.3 %copy-start.1 = (bf16[768,768]{1,0:T(8,128)(2,1)S(1)}, bf16[768,768]{1,0:T(8,128)(2,1)}, u32[]{:S(2)}) copy-start(bf16[768,768]{1,0:T(8,128)(2,1)} %param.6) | copy-start | bytes 3538948
  96.1 23.9 %all-to-all-start.5 = ((bf16[8,8,1536]{2,1,0:T(8,128)(2,1)}), bf16[8,8,1536]{2,1,0:T(8,128)(2,1)S(1)}, u32[]{:S(2)}, u32[]{:S(2)}) async-start(bf16[8,8,1536]{2,1,0:T(8,128)(2,1)} %bitcast.17), calls=%async_computation.5 | async-start | bytes 393216 | tf_op jit(solution)/shard_map/all_to_all | solution.py:32

commit v6 on v5

--- a/solution.py
+++ b/solution.py
@@ -7,7 +7,7 @@
 HIDDEN = ("y", "x_hi", "core")
 ORDER = ("core", "y", "x_hi")
 NEAR = ("x_lo", "z_near")
-FAR = ("z_far",)
+FAR = ("z2", "z4", "z8")
 C = 0.7978845608028654
 
 
@@ -63,8 +63,8 @@
 
 
 def solution(mesh):
-    fine = Mesh(mesh.devices.reshape(2, -1, 2, mesh.shape["row"], 2, 2), ("x_lo", "z_far", "z_near", "y", "x_hi", "core"))
-    wide = ("x_lo", "z_far", "z_near")
+    fine = Mesh(mesh.devices.reshape(2, 2, 2, 2, 2, mesh.shape["row"], 2, 2), ("x_lo", "z8", "z4", "z2", "z_near", "y", "x_hi", "core"))
+    wide = ("x_lo", "z8", "z4", "z2", "z_near")
     specs = (P(wide, HIDDEN), P(HIDDEN, wide), P(wide, HIDDEN), P(wide, HIDDEN))
     outs = (P(wide, HIDDEN), P(wide, HIDDEN), P(HIDDEN, wide), P(wide, HIDDEN))
     return jax.shard_map(per_device, mesh=fine, in_specs=specs, out_specs=outs, check_vma=False)

time: 122 us -> 120 us (0.984)
  the two profiles are of different devices: /device:TPU:24 before, /device:TPU:32 now
where the time goes in v6:
time: 120 us
  blocking collectives  89.1 us (74%)
  waiting for transfers between devices  13 us (11%)
  starting transfers between devices  8.86 us (7%)
  matrix products  5.02 us (4%)
  other arithmetic  2.05 us (2%)
    all_to_all x3, blocking collectives, gather(): lax.all_to_all(copies, axes, 0, 0, tiled=True).reshape(-1, rows.shape[1])  53 us
    all_to_all x2, blocking collectives, spread_sum(): lax.all_to_all(blocks, axes, 0, 0, tiled=True).astype(jnp.float32)  31.4 us
    all_to_all x1, waiting for transfers between devices, spread_sum(): lax.all_to_all(blocks, axes, 0, 0, tiled=True).astype(jnp.float32)  13 us
    all_to_all x1, starting transfers between devices, spread_sum(): lax.all_to_all(blocks, axes, 0, 0, tiled=True).astype(jnp.float32)  8.86 us
    dot_general x6, matrix products, dot(): lax.dot_general(left, right, (dims, ((), ())), preferred_element_type=jnp...  5.02 us
  transfers between devices with their start and end apart: 1, of which 1 were waited for; matrix products, arithmetic and copies ran while one was open for 3% of the time, Pallas kernels for 0%

profile of v6, /device:TPU:32, one launch (start us, length us, event | category | flops | bytes accessed | tf_op | source)
XLA Modules:
  0.0 119.6 jit_solution(13659214438160016093)
XLA Ops:
  0.6 0.0 copy-start
  0.7 0.8 pad_maximum_fusion.4
  1.5 29.2 %all_to_all.30 = bf16[8,8,1536]{2,1,0:T(8,128)(2,1)S(1)} all-to-all(bf16[8,8,1536]{2,1,0:T(8,128)(2,1)S(1)} %broadcast_in_dim.8), channel_id=1, replica_groups=mesh['x_lo'=2,'z8'=2,'z4'=2,'z2'=2,'z_near'=2,'y'=4,'x_hi'=2,'core'=2] {..., dimensions={0} | all-to-all | bytes 393216 | tf_op jit(solution)/shard_map/all_to_all | solution.py:27
  30.7 0.0 copy-start.1
  30.7 0.1 broadcast_in_dim.10
  30.8 11.6 %all_to_all.31 = bf16[4,64,1536]{2,1,0:T(8,128)(2,1)S(1)} all-to-all(bf16[4,64,1536]{2,1,0:T(8,128)(2,1)S(1)} %broadcast_in_dim.10), channel_id=1, replica_groups=mesh['x_lo'=2,'z8'=2,'z4'=2,'z2'=2,'z_near'=2,'y'=4,'x_hi'=2,'core'=2] {..., dimensions={0} | all-to-all | bytes 1572864 | tf_op jit(solution)/shard_map/all_to_all | solution.py:27
  42.4 0.0 copy-done.1
  42.4 0.5 fusion.5
  42.9 0.0 copy-done
  42.9 0.5 fusion.8
  43.4 0.1 fusion.17
  43.5 0.1 select_convert_fusion
  43.6 2.4 %all_gather.6 = bf16[256,1536]{1,0:T(8,128)(2,1)S(1)} all-gather(bf16[128,1536]{1,0:T(8,128)(2,1)S(1)} %select_convert_fusion), channel_id=1, replica_groups=mesh['x_lo'=2,'z8'=2,'z4'=2,'z2'=2,'z_near'=2,'y'=4,'x_hi'=2,'core'=2] {..., dimensions={0}, use_global_device_ids=true | all-gather | bytes 1179648 | tf_op jit(solution)/shard_map/all_gather | solution.py:47
  45.9 0.1 add_convert_fusion
  46.1 17.0 %all_to_all.32 = bf16[8,16,1536]{2,1,0:T(8,128)(2,1)S(1)} all-to-all(bf16[8,16,1536]{2,1,0:T(8,128)(2,1)S(1)} %bitcast.16), channel_id=1, replica_groups=mesh['x_lo'=2,'z8'=2,'z4'=2,'z2'=2,'z_near'=2,'y'=4,'x_hi'=2,'core'=2] {..., dimensions={0} | all-to-all | bytes 786432 | tf_op jit(solution)/shard_map/all_to_all | solution.py:32
  63.1 0.1 convert_reduce_fusion
  63.3 12.2 %all_to_all.33 = bf16[8,16,1536]{2,1,0:T(8,128)(2,1)S(1)} all-to-all(bf16[8,16,1536]{2,1,0:T(8,128)(2,1)S(1)} %broadcast_in_dim.22), channel_id=1, replica_groups=mesh['x_lo'=2,'z8'=2,'z4'=2,'z2'=2,'z_near'=2,'y'=4,'x_hi'=2,'core'=2] {..., dimensions={0} | all-to-all | bytes 786432 | tf_op jit(solution)/shard_map/all_to_all | solution.py:27
  75.5 2.4 %all_gather.7 = bf16[256,1536]{1,0:T(8,128)(2,1)S(1)} all-gather(bf16[128,1536]{1,0:T(8,128)(2,1)S(1)} %bitcast.15), channel_id=1, replica_groups=mesh['x_lo'=2,'z8'=2,'z4'=2,'z2'=2,'z_near'=2,'y'=4,'x_hi'=2,'core'=2] {..., dimensions={0}, use_global_device_ids=true | all-gather | bytes 1179648 | tf_op jit(solution)/shard_map/all_gather | solution.py:53
  77.9 0.5 convolution_convert_fusion.2
  78.4 0.5 convolution_convert_fusion.3
  78.9 0.1 pad_maximum_fusion.2
  78.9 14.3 %all_to_all.34 = bf16[4,64,1536]{2,1,0:T(8,128)(2,1)S(1)} all-to-all(bf16[4,64,1536]{2,1,0:T(8,128)(2,1)S(1)} %bitcast.14), channel_id=1, replica_groups=mesh['x_lo'=2,'z8'=2,'z4'=2,'z2'=2,'z_near'=2,'y'=4,'x_hi'=2,'core'=2] {..., dimensions={0} | all-to-all | bytes 1572864 | tf_op jit(solution)/shard_map/all_to_all | solution.py:32
  93.2 0.8 reduce_sum.34
  94.1 8.9 %all-to-all-start.5 = ((bf16[8,8,1536]{2,1,0:T(8,128)(2,1)}), bf16[8,8,1536]{2,1,0:T(8,128)(2,1)S(1)}, u32[]{:S(2)}, u32[]{:S(2)}) async-start(bf16[8,8,1536]{2,1,0:T(8,128)(2,1)} %bitcast.17), calls=%async_computation.5 | async-start | bytes 393216 | tf_op jit(solution)/shard_map/all_to_all | solution.py:32
  102.9 1.5 %convolution_convert_fusion = bf16[768,768]{1,0:T(8,128)(2,1)} fusion(bf16[256,1536]{1,0:T(8,128)(2,1)S(1)} %all_gather.7, bf16[256,1536]{1,0:T(8,128)(2,1)S(1)} %bitcast.12), kind=kOutput, calls=%fused_computation | convolution fusion | flops 302579712 | bytes 1966080 | tf_op jit(solution)/shard_map/dot_general | solution.py:22
  104.4 1.5 %convolution_convert_fusion.1 = bf16[768,768]{1,0:T(8,128)(2,1)} fusion(bf16[256,1536]{1,0:T(8,128)(2,1)S(1)} %all_gather.7, bf16[256,1536]{1,0:T(8,128)(2,1)S(1)} %bitcast.13), kind=kOutput, calls=%fused_computation.1 | convolution fusion | flops 302579712 | bytes 1966080 | tf_op jit(solution)/shard_map/dot_general | solution.py:22
  106.0 13.0 %all-to-all-done.5 = bf16[8,8,1536]{2,1,0:T(8,128)(2,1)S(1)} async-done(((bf16[8,8,1536]{2,1,0:T(8,128)(2,1)}), bf16[8,8,1536]{2,1,0:T(8,128)(2,1)S(1)}, u32[]{:S(2)}, u32[]{:S(2)}) %all-to-all-start.5) | async-done | bytes 196640 | tf_op jit(solution)/shard_map/all_to_all | solution.py:32
  119.0 0.6 fusion.19
  (5 shorter events, 0.1 us)
Async XLA Ops:
  0.6 42.2 %copy-start = (bf16[768,768]{1,0:T(8,128)(2,1)S(1)}, bf16[768,768]{1,0:T(8,128)(2,1)}, u32[]{:S(2)}) copy-start(bf16[768,768]{1,0:T(8,128)(2,1)} %param.5) | copy-start | bytes 3538948
  30.7 11.6 %copy-start.1 = (bf16[768,768]{1,0:T(8,128)(2,1)S(1)}, bf16[768,768]{1,0:T(8,128)(2,1)}, u32[]{:S(2)}) copy-start(bf16[768,768]{1,0:T(8,128)(2,1)} %param.6) | copy-start | bytes 3538948
  94.1 24.9 %all-to-all-start.5 = ((bf16[8,8,1536]{2,1,0:T(8,128)(2,1)}), bf16[8,8,1536]{2,1,0:T(8,128)(2,1)S(1)}, u32[]{:S(2)}, u32[]{:S(2)}) async-start(bf16[8,8,1536]{2,1,0:T(8,128)(2,1)} %bitcast.17), calls=%async_computation.5 | async-start | bytes 393216 | tf_op jit(solution)/shard_map/all_to_all | solution.py:32

commit v7 on v3

--- a/solution.py
+++ b/solution.py
@@ -7,7 +7,7 @@
 HIDDEN = ("y", "x_hi", "core")
 ORDER = ("core", "y", "x_hi")
 NEAR = ("x_lo", "z_near")
-FAR = ("z_far",)
+FAR = ("z2", "z4", "z8")
 C = 0.7978845608028654
 
 
@@ -57,8 +57,8 @@
 
 
 def solution(mesh):
-    fine = Mesh(mesh.devices.reshape(2, -1, 2, mesh.shape["row"], 2, 2), ("x_lo", "z_far", "z_near", "y", "x_hi", "core"))
-    wide = ("x_lo", "z_far", "z_near")
+    fine = Mesh(mesh.devices.reshape(2, 2, 2, 2, 2, mesh.shape["row"], 2, 2), ("x_lo", "z8", "z4", "z2", "z_near", "y", "x_hi", "core"))
+    wide = ("x_lo", "z8", "z4", "z2", "z_near")
     specs = (P(wide, HIDDEN), P(HIDDEN, wide), P(wide, HIDDEN), P(wide, HIDDEN))
     outs = (P(wide, HIDDEN), P(wide, HIDDEN), P(HIDDEN, wide), P(wide, HIDDEN))
     return jax.shard_map(per_device, mesh=fine, in_specs=specs, out_specs=outs, check_vma=False)

time: 125 us -> 123 us (0.984)
  the two profiles are of different devices: /device:TPU:24 before, /device:TPU:32 now
where the time goes in v7:
time: 123 us; the launch traced here: 122 us
  blocking collectives  91.8 us (75%)
  waiting for transfers between devices  13 us (11%)
  starting transfers between devices  8.87 us (7%)
  matrix products  5.01 us (4%)
  other arithmetic  1.94 us (2%)
    all_to_all x3, blocking collectives, gather(): lax.all_to_all(copies, axes, 0, 0, tiled=True).reshape(-1, rows.shape[1])  53.5 us
    all_to_all x2, blocking collectives, spread_sum(): lax.all_to_all(blocks, axes, 0, 0, tiled=True).astype(jnp.float32)  36 us
    all_to_all x1, waiting for transfers between devices, spread_sum(): lax.all_to_all(blocks, axes, 0, 0, tiled=True).astype(jnp.float32)  13 us
    all_to_all x1, starting transfers between devices, spread_sum(): lax.all_to_all(blocks, axes, 0, 0, tiled=True).astype(jnp.float32)  8.87 us
    dot_general x6, matrix products, dot(): lax.dot_general(left, right, (dims, ((), ())), preferred_element_type=jnp...  5.01 us
  transfers between devices with their start and end apart: 1, of which 1 were waited for; matrix products, arithmetic and copies ran while one was open for 3% of the time, Pallas kernels for 0%

profile of v7, /device:TPU:32, one launch (start us, length us, event | category | flops | bytes accessed | tf_op | source)
XLA Modules:
  0.0 122.1 jit_solution(5775315673924739018)
XLA Ops:
  0.6 0.0 copy-start
  0.6 0.8 pad_maximum_fusion.3
  1.5 29.2 %all_to_all.30 = bf16[8,8,1536]{2,1,0:T(8,128)(2,1)S(1)} all-to-all(bf16[8,8,1536]{2,1,0:T(8,128)(2,1)S(1)} %broadcast_in_dim.8), channel_id=1, replica_groups=mesh['x_lo'=2,'z8'=2,'z4'=2,'z2'=2,'z_near'=2,'y'=4,'x_hi'=2,'core'=2] {..., dimensions={0} | all-to-all | bytes 393216 | tf_op jit(solution)/shard_map/all_to_all | solution.py:27
  30.7 0.0 copy-start.1
  30.7 0.1 broadcast_in_dim.10
  30.8 11.6 %all_to_all.31 = bf16[4,64,1536]{2,1,0:T(8,128)(2,1)S(1)} all-to-all(bf16[4,64,1536]{2,1,0:T(8,128)(2,1)S(1)} %broadcast_in_dim.10), channel_id=1, replica_groups=mesh['x_lo'=2,'z8'=2,'z4'=2,'z2'=2,'z_near'=2,'y'=4,'x_hi'=2,'core'=2] {..., dimensions={0} | all-to-all | bytes 1572864 | tf_op jit(solution)/shard_map/all_to_all | solution.py:27
  42.4 0.0 copy-done.1
  42.4 0.5 convolution_convert_fusion.4
  42.9 0.0 copy-done
  42.9 0.5 convolution_convert_fusion.5
  43.4 0.1 pad_maximum_fusion
  43.4 21.7 %all_to_all.32 = bf16[16,16,1536]{2,1,0:T(8,128)(2,1)S(1)} all-to-all(bf16[16,16,1536]{2,1,0:T(8,128)(2,1)S(1)} %bitcast.10), channel_id=1, replica_groups=mesh['x_lo'=2,'z8'=2,'z4'=2,'z2'=2,'z_near'=2,'y'=4,'x_hi'=2,'core'=2] {..., dimensions={0} | all-to-all | bytes 1572864 | tf_op jit(solution)/shard_map/all_to_all | solution.py:32
  65.1 0.1 convert_reduce_fusion
  65.3 12.7 %all_to_all.33 = bf16[8,16,1536]{2,1,0:T(8,128)(2,1)S(1)} all-to-all(bf16[8,16,1536]{2,1,0:T(8,128)(2,1)S(1)} %broadcast_in_dim.22), channel_id=1, replica_groups=mesh['x_lo'=2,'z8'=2,'z4'=2,'z2'=2,'z_near'=2,'y'=4,'x_hi'=2,'core'=2] {..., dimensions={0} | all-to-all | bytes 786432 | tf_op jit(solution)/shard_map/all_to_all | solution.py:27
  78.0 2.4 %all_gather.3 = bf16[256,1536]{1,0:T(8,128)(2,1)S(1)} all-gather(bf16[128,1536]{1,0:T(8,128)(2,1)S(1)} %bitcast.16), channel_id=1, replica_groups=mesh['x_lo'=2,'z8'=2,'z4'=2,'z2'=2,'z_near'=2,'y'=4,'x_hi'=2,'core'=2] {..., dimensions={0}, use_global_device_ids=true | all-gather | bytes 1179648 | tf_op jit(solution)/shard_map/all_gather | solution.py:47
  80.3 0.5 convolution_convert_fusion.2
  80.9 0.5 convolution_convert_fusion.3
  81.3 0.1 pad_maximum_fusion.1
  81.4 14.3 %all_to_all.34 = bf16[4,64,1536]{2,1,0:T(8,128)(2,1)S(1)} all-to-all(bf16[4,64,1536]{2,1,0:T(8,128)(2,1)S(1)} %bitcast.11), channel_id=1, replica_groups=mesh['x_lo'=2,'z8'=2,'z4'=2,'z2'=2,'z_near'=2,'y'=4,'x_hi'=2,'core'=2] {..., dimensions={0} | all-to-all | bytes 1572864 | tf_op jit(solution)/shard_map/all_to_all | solution.py:32
  95.7 0.8 reduce_sum.34
  96.5 8.9 %all-to-all-start.5 = ((bf16[8,8,1536]{2,1,0:T(8,128)(2,1)}), bf16[8,8,1536]{2,1,0:T(8,128)(2,1)S(1)}, u32[]{:S(2)}, u32[]{:S(2)}) async-start(bf16[8,8,1536]{2,1,0:T(8,128)(2,1)} %bitcast.17), calls=%async_computation.5 | async-start | bytes 393216 | tf_op jit(solution)/shard_map/all_to_all | solution.py:32
  105.4 1.5 %convolution_convert_fusion = bf16[768,768]{1,0:T(8,128)(2,1)} fusion(bf16[256,1536]{1,0:T(8,128)(2,1)S(1)} %all_gather.3, bf16[256,1536]{1,0:T(8,128)(2,1)S(1)} %bitcast.14), kind=kOutput, calls=%fused_computation.1 | convolution fusion | flops 302579712 | bytes 1966080 | tf_op jit(solution)/shard_map/dot_general | solution.py:22
  106.9 1.5 %convolution_convert_fusion.1 = bf16[768,768]{1,0:T(8,128)(2,1)} fusion(bf16[256,1536]{1,0:T(8,128)(2,1)S(1)} %all_gather.3, bf16[256,1536]{1,0:T(8,128)(2,1)S(1)} %bitcast.15), kind=kOutput, calls=%fused_computation.2 | convolution fusion | flops 302579712 | bytes 1966080 | tf_op jit(solution)/shard_map/dot_general | solution.py:22
  108.5 13.0 %all-to-all-done.5 = bf16[8,8,1536]{2,1,0:T(8,128)(2,1)S(1)} async-done(((bf16[8,8,1536]{2,1,0:T(8,128)(2,1)}), bf16[8,8,1536]{2,1,0:T(8,128)(2,1)S(1)}, u32[]{:S(2)}, u32[]{:S(2)}) %all-to-all-start.5) | async-done | bytes 196640 | tf_op jit(solution)/shard_map/all_to_all | solution.py:32
  121.5 0.6 fusion.15
  (5 shorter events, 0.1 us)
Async XLA Ops:
  0.6 42.2 %copy-start = (bf16[768,768]{1,0:T(8,128)(2,1)S(1)}, bf16[768,768]{1,0:T(8,128)(2,1)}, u32[]{:S(2)}) copy-start(bf16[768,768]{1,0:T(8,128)(2,1)} %param.5) | copy-start | bytes 3538948
  30.7 11.6 %copy-start.1 = (bf16[768,768]{1,0:T(8,128)(2,1)S(1)}, bf16[768,768]{1,0:T(8,128)(2,1)}, u32[]{:S(2)}) copy-start(bf16[768,768]{1,0:T(8,128)(2,1)} %param.6) | copy-start | bytes 3538948
  96.5 24.9 %all-to-all-start.5 = ((bf16[8,8,1536]{2,1,0:T(8,128)(2,1)}), bf16[8,8,1536]{2,1,0:T(8,128)(2,1)S(1)}, u32[]{:S(2)}, u32[]{:S(2)}) async-start(bf16[8,8,1536]{2,1,0:T(8,128)(2,1)} %bitcast.17), calls=%async_computation.5 | async-start | bytes 393216 | tf_op jit(solution)/shard_map/all_to_all | solution.py:32
